TPU v7x, 512 devices: a whole 4x8x8 slice. The times are simulated.
512 devices in a mesh: row: 16 (over y_hi, x, core), col: 32 (over y_lo, z).
Axes of the slice: x: 4, y: 8 (y_hi: 2, y_lo: 4; y = y_hi * 4 + y_lo), z: 8, core: 2. Of those that a mesh axis runs over, the one named last changes fastest.
Arguments:
- samples: bfloat16 [256, 16384], P('row', 'col'), may hold values from -40 to 40
- counts: int32 [256], replicated, may hold values from 1 to 64
- shrink_num: int32 [1], replicated, may hold values from 20 to 60
- shrink_den: int32 [1], replicated, may hold values from 100 to 128
Outputs:
- factored: float32 [2, 8192, 16384], P(None, 'row', 'col')
All inputs are finite; a program needn't handle non-finite values.
Results may differ from a plain program's by a relative error of at most 0.0048.
Values may be sent and summed in bfloat16 or wider, within the bound.
No kernel may reach another device: no remote copies, remote signals or barrier semaphores. Data moves between devices by JAX's collectives and lax.ppermute only.
A program may use at most 64 MiB of HBM per device.

v0:
```python
import jax
import jax.numpy as jnp
from jax import lax
from jax.sharding import PartitionSpec as P


def broadcast(value, axis, source):
    kept = jnp.where(lax.axis_index(axis) == source, value, 0).astype(value.dtype)
    return lax.psum(kept, axis)


def solve_right(lower_factor, tile):
    return lax.linalg.triangular_solve(
        lower_factor, tile, left_side=False, lower=True, transpose_a=True
    )


def product(left, right):
    return lax.dot_general(
        left, right, (((0,), (0,)), ((), ())), preferred_element_type=jnp.float32
    )


def per_device(samples, counts, shrink_num, shrink_den):
    rows_count = lax.axis_size("row")
    cols_count = lax.axis_size("col")
    ratio = cols_count // rows_count
    row_index = lax.axis_index("row")
    col_index = lax.axis_index("col")
    width = samples.shape[1]
    gathered = lax.all_gather(samples, "row", axis=0, tiled=True)
    weights = counts.astype(jnp.float32) / jnp.sum(counts.astype(jnp.float32))
    shrinkage = shrink_num[0].astype(jnp.float32) / shrink_den[0].astype(jnp.float32)
    values = gathered.astype(jnp.float32)
    mean = jnp.sum(weights[:, None] * values, axis=0)
    scaled = (jnp.sqrt(weights)[:, None] * (values - mean)).astype(jnp.bfloat16)
    block_rows = [position * rows_count + row_index for position in range(ratio)]
    operands = []
    grams = []
    for position in range(ratio):
        operand = broadcast(scaled, "col", position * rows_count + row_index)
        operands.append(operand)
        grams.append(product(operand, scaled))
    partial_trace = jnp.float32(0.0)
    for position in range(ratio):
        partial_trace = partial_trace + jnp.where(
            block_rows[position] == col_index, jnp.trace(grams[position]), 0.0
        )
    total = lax.psum(partial_trace, ("row", "col"))
    level = shrinkage * total / (width * cols_count)
    identity = jnp.eye(width, dtype=jnp.float32)
    tiles = jnp.stack(
        [
            (1.0 - shrinkage) * grams[position]
            + jnp.where(block_rows[position] == col_index, level, 0.0) * identity
            for position in range(ratio)
        ]
    )
    row_ids = jnp.stack(block_rows)[:, None, None]
    on_column = col_index == 0
    diagonal_tile = (1.0 - shrinkage) * product(scaled, scaled) + level * identity
    diag_factor = jnp.linalg.cholesky(jnp.where(on_column, diagonal_tile, identity))
    below = jnp.stack([solve_right(diag_factor, tiles[position]) for position in range(ratio)])
    panel = jnp.where(row_ids > 0, below, diag_factor[None])
    received = broadcast(panel, "col", 0)
    selected = lax.dynamic_index_in_dim(received, col_index // rows_count, 0, keepdims=False)
    partner = broadcast(selected, "row", col_index % rows_count)
    update = jnp.einsum("sab,cb->sac", received, partner, precision=lax.Precision.HIGHEST)
    trailing = (row_ids > 0) & (col_index > 0)
    tiles = jnp.where(trailing, tiles - update, tiles)
    tiles = jnp.where(on_column, received, tiles)
    tiles = jnp.where((row_ids == 0) & (col_index > 0), 0.0, tiles)
    return tiles


def solution(mesh):
    in_specs = (P("row", "col"), P(), P(), P())
    out_specs = P(None, "row", "col")
    return jax.shard_map(
        per_device, mesh=mesh, in_specs=in_specs, out_specs=out_specs, check_vma=False
    )
```

profile of v0, /device:TPU:1, one launch (start us, length us, event | category | flops | bytes accessed | tf_op | source)
XLA Modules:
  0.0 1109.0 jit_solution(3195803003528372530)
XLA Ops:
  7.8 1.3 fusion.65
  9.2 34.1 %all_gather.3 = bf16[256,512]{1,0:T(8,128)(2,1)S(1)} all-gather(bf16[16,512]{1,0:T(8,128)(2,1)} %param.6), channel_id=1, replica_groups=mesh['row'=16,'col'=32] {'row'}, dimensions={0}, use_global_device_ids=true | all-gather | bytes 278528 | tf_op jit(solution)/shard_map/all_gather | solution.py:31
  45.9 281.4 %all-reduce.10.cloned.1.call-done = (bf16[256,512]{1,0:T(8,128)(2,1)}, bf16[256,512]{1,0:T(8,128)(2,1)}) async-done(((bf16[256,512]{1,0:T(8,128)(2,1)}, bf16[256,512]{1,0:T(8,128)(2,1)}), (bf16[256,512]{1,0:T(8,128)(2,1)}, bf16[256,512]{1,0:T(8,128)(2,1)})) %all-reduce.10.cloned.1.call-update) | async-done | bytes 524304 | tf_op jit(solution)/shard_map/psum | solution.py:9
  327.3 3.0 select_reduce_fusion
  330.3 3.0 select_reduce_fusion.1
  334.7 117.3 %psum.37 = f32[]{:T(128)} all-reduce(f32[]{:T(128)S(6)} %add.78), channel_id=1, replica_groups=mesh['row'=16,'col'=32] {'row','col'}, use_global_device_ids=true, to_apply=%region_6.7 | all-reduce | flops 1 | bytes 8 | tf_op jit(solution)/shard_map/psum | solution.py:49
  453.7 11.7 %cholesky.103 = f32[128,128]{1,0:T(8,128)S(1)} custom-call(f32[128,128]{1,0:T(8,128)S(1)} %cholesky.263), custom_call_target="Cholesky" | custom-call | tf_op jit(solution)/shard_map/jit(cholesky)/cholesky | solution.py:62
  465.6 9.8 custom-call.30
  476.2 11.7 %cholesky.215 = f32[128,128]{1,0:T(8,128)S(1)} custom-call(f32[128,128]{1,0:T(8,128)S(1)} %cholesky.267), custom_call_target="Cholesky" | custom-call | tf_op jit(solution)/shard_map/jit(cholesky)/cholesky | solution.py:62
  488.1 10.0 custom-call.31
  499.1 11.7 %cholesky.236 = f32[128,128]{1,0:T(8,128)S(1)} custom-call(f32[128,128]{1,0:T(8,128)S(1)} %cholesky.272), custom_call_target="Cholesky" | custom-call | tf_op jit(solution)/shard_map/jit(cholesky)/cholesky | solution.py:62
  511.0 9.8 custom-call.32
  521.6 11.9 %cholesky.253 = f32[128,128]{1,0:T(8,128)S(1)} custom-call(f32[128,128]{1,0:T(8,128)S(1)} %convolution_subtract_fusion.8), custom_call_target="Cholesky" | custom-call | tf_op jit(solution)/shard_map/jit(cholesky)/cholesky | solution.py:62
  539.5 10.9 while.4
  542.9 1.3 dynamic-slice.9
  548.3 1.3 dynamic-slice.9
  550.4 40.1 %custom-call.34 = f32[4,128,128]{1,2,0:T(8,128)S(1)} custom-call(f32[4,128,128]{2,1,0:T(8,128)} %get-tuple-element.20), custom_call_target="InvertDiagBlocksLowerTriangular" | custom-call | tf_op jit(solution)/shard_map/triangular_solve/custom-call.3 | solution.py:13
  590.5 1.8 select_add_fusion
  599.1 1.7 fusion.2
  601.2 285.1 %all-reduce.6.cloned.1.call-done = f32[2,512,512]{1,2,0:T(8,128)} async-done(((f32[2,512,512]{1,2,0:T(8,128)}), f32[2,512,512]{1,2,0:T(8,128)}) %all-reduce.6.cloned.1.call-update) | async-done | bytes 2097168 | tf_op jit(solution)/shard_map/psum | solution.py:9
  886.3 2.3 select_bitcast_fusion
  888.7 202.9 %all-reduce.8.cloned.1.call-done = f32[512,512]{0,1:T(8,128)} async-done(((f32[512,512]{0,1:T(8,128)}), f32[512,512]{0,1:T(8,128)}) %all-reduce.8.cloned.1.call-update) | async-done | bytes 1048592 | tf_op jit(solution)/shard_map/psum | solution.py:9
  1091.6 7.5 fusion.1
  1099.1 2.9 copy.26
  (80 shorter events, 25.2 us)
Async XLA Ops:
  6.5 320.8 %all-reduce.10.cloned.1.call-start = ((), (), s32[]{:S(2)}) async-start(), calls=%async_computation.2 | async-start | bytes 1048576 | tf_op jit(solution)/shard_map/psum | solution.py:9
  44.4 842.0 %all-reduce.6.cloned.1.call-start = ((), (), s32[]{:S(2)}) async-start(), calls=%async_computation | async-start | bytes 4194304 | tf_op jit(solution)/shard_map/psum | solution.py:9
  597.9 1.2 copy-start
  600.9 490.7 %all-reduce.8.cloned.1.call-start = ((), (), s32[]{:S(2)}) async-start(), calls=%async_computation.1 | async-start | bytes 2097152 | tf_op jit(solution)/shard_map/psum | solution.py:9
Sparse Core Ops, SparseCore 0:
  44.5 282.7 all-reduce.9
  601.0 285.2 all-reduce.5
  889.3 202.3 all-reduce.7
where the time goes:
time: 1120 us; the launch traced here: 1110 us
  waiting for transfers between devices  770 us (69%)
  blocking collectives  151 us (13%)
  other arithmetic  130 us (12%)
  matrix products  22.8 us (2%)
  between operations  19.9 us (2%)
  local copies, waits for them, and re-layouts  14.7 us (1%)
    psum x3, waiting for transfers between devices, broadcast(): return lax.psum(kept, axis)  769 us
    psum x1, blocking collectives, per_device(): total = lax.psum(partial_trace, ('row', 'col'))  117 us
    another operation x14, other arithmetic, per_device(): jnp.linalg.cholesky(jnp.where(on_column, diagonal_tile, identity))  78.8 us
    another operation x4, other arithmetic, solve_right(): lax.linalg.triangular_solve(lower_factor, tile, left_side=False, lower=Tr...  41.4 us
    all_gather x1, blocking collectives, per_device(): gathered = lax.all_gather(samples, 'row', axis=0, tiled=True)  34.1 us
  transfers between devices with their start and end apart: 3, of which 3 were waited for; matrix products, arithmetic and copies ran while one was open for 0% of the time, Pallas kernels for 0%

commit v1 on v0

v1 whole, which is shorter than its diff:
```python
import functools

import jax
import jax.numpy as jnp
from jax import lax
from jax.experimental import pallas as pl
from jax.experimental.pallas import tpu as pltpu
from jax.sharding import PartitionSpec as P

BLOCK = 128
MICRO = 32
F32 = jnp.float32
BF16 = jnp.bfloat16
VMEM = pl.BlockSpec(memory_space=pltpu.VMEM)
SMEM = pl.BlockSpec(memory_space=pltpu.SMEM)


def dot(left, right, dims, precision=None):
    return lax.dot_general(
        left, right, ((dims[0], dims[1]), ((), ())),
        precision=precision, preferred_element_type=F32,
    )


def exact_dot(left, right, dims):
    return dot(left, right, dims, lax.Precision.HIGHEST)


def split(value):
    high = value.astype(BF16)
    return high, (value - high.astype(F32)).astype(BF16)


def scale_kernel(place_ref, counts_ref, samples_ref, scaled_ref, pieces_ref):
    count, rows, width = samples_ref.shape
    number = count * rows
    counts = counts_ref[...].astype(F32)
    weights = jnp.broadcast_to(counts / jnp.sum(counts), (8, number))
    column = jnp.transpose(weights)[:, 0:1]
    values = samples_ref[...].reshape(number, width).astype(F32)
    mean = jnp.sum(column * values, axis=0, keepdims=True)
    scaled = (jnp.sqrt(column) * (values - mean)).astype(BF16)
    scaled_ref[...] = scaled
    share = jnp.sum(jnp.square(scaled.astype(F32)), axis=0, keepdims=True)
    share = jnp.broadcast_to(jnp.sum(share, axis=1, keepdims=True), (rows, 128))
    high, rest = split(share)
    middle = rest
    low = (share - high.astype(F32) - middle.astype(F32)).astype(BF16)
    line = lax.broadcasted_iota(jnp.int32, (rows, 128), 0)
    tail = jnp.where(line == 0, high.astype(F32), 0.0)
    tail = jnp.where(line == 1, middle.astype(F32), tail)
    tail = jnp.where(line == 2, low.astype(F32), tail).astype(BF16)
    first = pl.multiple_of(place_ref[0] * rows, rows)
    own = scaled_ref[pl.ds(first, rows), :]
    for target in range(pieces_ref.shape[0]):
        pieces_ref[target, :, 0:width] = own
        pieces_ref[target, :, width:] = tail


def deal_kernel(pieces_ref, dealt_ref, trace_ref):
    columns, rows, _ = pieces_ref.shape
    targets, _, width = dealt_ref.shape
    for target in range(targets):
        dealt_ref[target, 0:rows, :] = pieces_ref[0, :, 0:width]
        for position in range(columns // targets):
            tile = position * targets + target
            dealt_ref[target, (position + 1) * rows:(position + 2) * rows, :] = pieces_ref[tile, :, 0:width]
    tails = pieces_ref[:, :, width:].reshape(columns * rows, 128).astype(F32)
    total = jnp.sum(tails, axis=0, keepdims=True)
    trace_ref[...] = jnp.broadcast_to(total, (8, 128))


def eliminate(work_ref, first, micro):
    lanes = work_ref.shape[1]
    groups = micro // 8
    rows = [[work_ref[first + 8 * g:first + 8 * g + 8, 128 * w:128 * w + 128] for w in range(lanes // 128)] for g in range(groups)]
    part, lane = first // 128, first % 128
    columns = [
        [jnp.broadcast_to(rows[g][part][:, lane + k:lane + k + 1], (8, 128)) for g in range(groups)] for k in range(micro)
    ]
    for j in range(micro):
        group, line = j // 8, j % 8

        def spread(value):
            return jnp.broadcast_to(value[line:line + 1, :], (8, 128))

        scale = lax.rsqrt(spread(columns[j][group]))
        multiplier = [columns[j][g] * scale for g in range(groups)]
        for k in range(j + 1, micro):
            pivot = spread(columns[k][group]) * scale
            for g in range((j + 1) // 8, groups):
                columns[k][g] = columns[k][g] - multiplier[g] * pivot
        for w in range(lanes // 128):
            pivot = spread(rows[group][w]) * scale
            work_ref[first + j:first + j + 1, 128 * w:128 * w + 128] = pivot[0:1, :]
            for g in range((j + 1) // 8, groups):
                rows[g][w] = rows[g][w] - multiplier[g] * pivot


def factor_block(work_ref, block, micro):
    for first in range(0, block, micro):
        eliminate(work_ref, first, micro)
        after = first + micro
        if after < block:
            panel = work_ref[first:after, :]
            work_ref[after:, :] = work_ref[after:, :] - exact_dot(panel[:, after:block], panel, ((0,), (0,)))


def identity(size):
    return jnp.where(
        lax.broadcasted_iota(jnp.int32, (size, size), 0) == lax.broadcasted_iota(jnp.int32, (size, size), 1), 1.0, 0.0
    ).astype(F32)


def factor_kernel(place_ref, shrink_ref, trace_ref, scaled_ref, dealt_ref, out_ref, panel_ref, work_ref):
    sources, dealt_rows, width = dealt_ref.shape
    samples = scaled_ref.shape[0]
    rows = samples // sources
    positions = out_ref.shape[0]
    row_index, col_index, taps = place_ref[0], place_ref[1], place_ref[2]
    shrinkage = shrink_ref[0].astype(F32) / shrink_ref[1].astype(F32)
    keep = 1.0 - shrinkage
    level = shrinkage * trace_ref[0:1, 0:1] / taps.astype(F32)
    first_tile = dealt_ref[:, 0:rows, :].reshape(samples, width)
    panel_ref[:, 0:width] = keep * dot(first_tile, first_tile, ((0,), (0,))) + level * identity(width)
    panel_ref[:, width:] = jnp.transpose(first_tile.astype(F32))
    for start in range(0, width, BLOCK):
        stop = start + BLOCK
        work_ref[:, 0:BLOCK] = panel_ref[start:stop, start:stop]
        work_ref[:, BLOCK:] = identity(BLOCK)
        factor_block(work_ref, BLOCK, MICRO)
        panel_ref[start:stop, start:stop] = work_ref[:, 0:BLOCK]
        done = exact_dot(work_ref[:, BLOCK:], panel_ref[start:stop, stop:], ((1,), (0,)))
        panel_ref[start:stop, stop:] = done
        if stop < width:
            panel_ref[stop:width, stop:] = panel_ref[stop:width, stop:] - exact_dot(done[:, 0:width - stop], done, ((0,), (0,)))
    reduced = panel_ref[:, width:]

    def finish(right):
        right_high, right_low = split(right)
        for position in range(positions):
            tile = dealt_ref[:, (position + 1) * rows:(position + 2) * rows, :].reshape(samples, width)
            product = dot(tile, right_high, ((0,), (0,))) + dot(tile, right_low, ((0,), (0,)))
            out_ref[position] = keep * product

    @pl.when(col_index == 0)
    def _():
        finish(jnp.transpose(reduced))

    @pl.when(col_index > 0)
    def _():
        high, low = split(reduced)
        inner = dot(high, high, ((0,), (0,))) + dot(high, low, ((0,), (0,))) + dot(low, high, ((0,), (0,)))
        inner_high, inner_low = split(inner)
        own = scaled_ref[...]
        removed = dot(inner_high, own, ((1,), (0,))) + dot(inner_low, own, ((1,), (0,)))
        finish(own.astype(F32) - keep * removed)
        for position in range(positions):
            @pl.when(position * sources + row_index == col_index)
            def _():
                out_ref[position] = out_ref[position] + level * identity(width)

    @pl.when((row_index == 0) & (col_index > 0))
    def _():
        out_ref[0] = jnp.zeros((width, width), F32)

    @pl.when((row_index == 0) & (col_index == 0))
    def _():
        upper = panel_ref[:, 0:width]
        line = lax.broadcasted_iota(jnp.int32, (width, width), 0)
        lane = lax.broadcasted_iota(jnp.int32, (width, width), 1)
        out_ref[0] = jnp.transpose(jnp.where(line <= lane, upper, 0.0))


def scale(place, counts, gathered, columns):
    count, rows, width = gathered.shape
    return pl.pallas_call(
        scale_kernel,
        out_shape=(
            jax.ShapeDtypeStruct((count * rows, width), BF16),
            jax.ShapeDtypeStruct((columns, rows, width + 128), BF16),
        ),
        in_specs=[SMEM, VMEM, VMEM],
        out_specs=(VMEM, VMEM),
        compiler_params=pltpu.CompilerParams(vmem_limit_bytes=32 * 2**20),
    )(place, counts[None, :], gathered)


def deal(pieces, targets):
    columns, rows, wide = pieces.shape
    return pl.pallas_call(
        deal_kernel,
        out_shape=(
            jax.ShapeDtypeStruct((targets, (1 + columns // targets) * rows, wide - 128), BF16),
            jax.ShapeDtypeStruct((8, 128), F32),
        ),
        in_specs=[VMEM],
        out_specs=(VMEM, VMEM),
        compiler_params=pltpu.CompilerParams(vmem_limit_bytes=32 * 2**20),
    )(pieces)


def factor(place, shrink, trace, scaled, dealt):
    samples, width = scaled.shape
    positions = dealt.shape[1] * dealt.shape[0] // samples - 1
    return pl.pallas_call(
        factor_kernel,
        out_shape=jax.ShapeDtypeStruct((positions, width, width), F32),
        in_specs=[SMEM, SMEM, VMEM, VMEM, VMEM],
        out_specs=VMEM,
        scratch_shapes=[
            pltpu.VMEM((width, width + samples), F32),
            pltpu.VMEM((BLOCK, 2 * BLOCK), F32),
        ],
        compiler_params=pltpu.CompilerParams(vmem_limit_bytes=48 * 2**20),
    )(place, shrink, trace, scaled, dealt)


def per_device(samples, counts, shrink_num, shrink_den):
    rows_count = lax.axis_size("row")
    cols_count = lax.axis_size("col")
    rows, width = samples.shape
    place = jnp.stack(
        [lax.axis_index("row"), lax.axis_index("col"), jnp.int32(width * cols_count)]
    ).astype(jnp.int32)
    shrink = jnp.concatenate([shrink_num, shrink_den])
    copies = jnp.broadcast_to(samples[None], (rows_count, rows, width))
    gathered = lax.all_to_all(copies, "row", 0, 0)
    scaled, pieces = scale(place, counts, gathered, cols_count)
    exchanged = lax.all_to_all(pieces, "col", 0, 0)
    dealt, trace = deal(exchanged, rows_count)
    dealt = lax.all_to_all(dealt, "row", 0, 0)
    return factor(place, shrink, trace, scaled, dealt)


def solution(mesh):
    in_specs = (P("row", "col"), P(), P(), P())
    out_specs = P(None, "row", "col")
    return jax.shard_map(
        per_device, mesh=mesh, in_specs=in_specs, out_specs=out_specs, check_vma=False
    )
```

time: 1120 us -> 112 us (0.10)
  the two profiles are of different devices: /device:TPU:1 before, /device:TPU:8 now
where the time goes in v1:
time: 112 us
  waiting for transfers between devices  39.3 us (35%)
  blocking collectives  30.6 us (27%)
  Pallas kernels  26.1 us (23%)
  starting transfers between devices  12.4 us (11%)
  local copies, waits for them, and re-layouts  2.12 us (2%)
  between operations  1.33 us (1%)
    all_to_all x1, blocking collectives, per_device(): exchanged = lax.all_to_all(pieces, 'col', 0, 0)  30.6 us
    all_to_all x1, waiting for transfers between devices, per_device(): dealt = lax.all_to_all(dealt, 'row', 0, 0)  24.6 us
    pallas_call x1, Pallas kernels, factor(): pl.pallas_call(factor_kernel, out_shape=jax.ShapeDtypeStruct((positions,...  24.1 us
    all_to_all x1, waiting for transfers between devices, per_device(): gathered = lax.all_to_all(copies, 'row', 0, 0)  14.7 us
    all_to_all x1, starting transfers between devices, per_device(): gathered = lax.all_to_all(copies, 'row', 0, 0)  8.77 us
    all_to_all x1, starting transfers between devices, per_device(): dealt = lax.all_to_all(dealt, 'row', 0, 0)  3.61 us
  transfers between devices with their start and end apart: 2, of which 2 were waited for; matrix products, arithmetic and copies ran while one was open for 0% of the time, Pallas kernels for 0%

profile of v1, /device:TPU:8, one launch (start us, length us, event | category | flops | bytes accessed | tf_op | source)
XLA Modules:
  0.0 112.0 jit_solution(13568142328705979821)
XLA Ops:
  0.0 1.4 %broadcast_in_dim.10 = bf16[16,16,512]{2,1,0:T(8,128)(2,1)} broadcast(bf16[16,512]{1,0:T(8,128)(2,1)} %param.4), dimensions={1,2} | broadcast | bytes 278528 | tf_op jit(solution)/shard_map/broadcast_in_dim | solution.py:227
  1.4 8.8 %all-to-all-start = ((bf16[16,16,512]{2,1,0:T(8,128)(2,1)}), bf16[16,16,512]{2,1,0:T(8,128)(2,1)S(1)}, u32[]{:S(2)}, u32[]{:S(2)}) async-start(bf16[16,16,512]{2,1,0:T(8,128)(2,1)} %broadcast_in_dim.10), calls=%async_computation | async-start | bytes 524288 | tf_op jit(solution)/shard_map/all_to_all | solution.py:228
  10.2 0.1 pad_add_fusion.place_ref
  10.3 14.7 %all-to-all-done.samples_ref = bf16[16,16,512]{2,1,0:T(8,128)(2,1)S(1)} async-done(((bf16[16,16,512]{2,1,0:T(8,128)(2,1)}), bf16[16,16,512]{2,1,0:T(8,128)(2,1)S(1)}, u32[]{:S(2)}, u32[]{:S(2)}) %all-to-all-start) | async-done | bytes 262176 | tf_op jit(solution)/shard_map/all_to_all | solution.py:228
  25.0 0.0 copy-start
  25.0 0.7 copy-done
  25.7 1.1 shard_map.46
  26.8 30.6 %all_to_all.15.pieces_ref = bf16[32,16,640]{2,1,0:T(8,128)(2,1)S(1)} all-to-all(bf16[32,16,640]{2,1,0:T(8,128)(2,1)S(1)} %get-tuple-element.9), channel_id=1, replica_groups=mesh['row'=16,'col'=32] {'col'}, dimensions={0} | all-to-all | bytes 1310720 | tf_op jit(solution)/shard_map/all_to_all | solution.py:230
  57.4 0.9 shard_map.47
  58.3 3.6 %all-to-all-start.2 = ((bf16[16,48,512]{2,1,0:T(8,128)(2,1)}), bf16[16,48,512]{2,1,0:T(8,128)(2,1)S(1)}, u32[]{:S(2)}, u32[]{:S(2)}) async-start(bf16[16,48,512]{2,1,0:T(8,128)(2,1)} %get-tuple-element.12), calls=%async_computation.2 | async-start | bytes 1572864 | tf_op jit(solution)/shard_map/all_to_all | solution.py:232
  63.2 0.1 pad_add_fusion.1.shrink_ref
  63.3 24.6 %all-to-all-done.2.dealt_ref = bf16[16,48,512]{2,1,0:T(8,128)(2,1)S(1)} async-done(((bf16[16,48,512]{2,1,0:T(8,128)(2,1)}), bf16[16,48,512]{2,1,0:T(8,128)(2,1)S(1)}, u32[]{:S(2)}, u32[]{:S(2)}) %all-to-all-start.2) | async-done | bytes 786464 | tf_op jit(solution)/shard_map/all_to_all | solution.py:232
  87.9 24.1 %shard_map.48 = f32[2,512,512]{2,1,0:T(8,128)} custom-call(s32[3]{0:T(128)S(1)} %pad_add_fusion.place_ref, s32[2]{0:T(128)S(1)} %pad_add_fusion.1.shrink_ref, f32[8,128]{1,0:T(8,128)S(1)} %get-tuple-element.10.trace_ref, bf16[256,512]{1,0:T(8,128)(2,1)S(1)} %get-tuple-element.11.scaled_ref, bf16[16,48,512]{2,1,0:T(8,128)(2,1)S(1)} %all-to-all-done.2.dealt_ref), custom_call_target="tpu_custom_call" | custom-call | tf_op jit(solution)/shard_map/pallas_call | solution.py:206
Async XLA Ops:
  1.4 23.5 %all-to-all-start = ((bf16[16,16,512]{2,1,0:T(8,128)(2,1)}), bf16[16,16,512]{2,1,0:T(8,128)(2,1)S(1)}, u32[]{:S(2)}, u32[]{:S(2)}) async-start(bf16[16,16,512]{2,1,0:T(8,128)(2,1)} %broadcast_in_dim.10), calls=%async_computation | async-start | bytes 524288 | tf_op jit(solution)/shard_map/all_to_all | solution.py:228
  25.0 0.7 copy-start
  58.3 29.6 %all-to-all-start.2 = ((bf16[16,48,512]{2,1,0:T(8,128)(2,1)}), bf16[16,48,512]{2,1,0:T(8,128)(2,1)S(1)}, u32[]{:S(2)}, u32[]{:S(2)}) async-start(bf16[16,48,512]{2,1,0:T(8,128)(2,1)} %get-tuple-element.12), calls=%async_computation.2 | async-start | bytes 1572864 | tf_op jit(solution)/shard_map/all_to_all | solution.py:232

commit v2 on v1

--- a/solution.py
+++ b/solution.py
@@ -1,5 +1,3 @@
-import functools
-
 import jax
 import jax.numpy as jnp
 from jax import lax
@@ -112,19 +110,8 @@
     ).astype(F32)
 
 
-def factor_kernel(place_ref, shrink_ref, trace_ref, scaled_ref, dealt_ref, out_ref, panel_ref, work_ref):
-    sources, dealt_rows, width = dealt_ref.shape
-    samples = scaled_ref.shape[0]
-    rows = samples // sources
-    positions = out_ref.shape[0]
-    row_index, col_index, taps = place_ref[0], place_ref[1], place_ref[2]
-    shrinkage = shrink_ref[0].astype(F32) / shrink_ref[1].astype(F32)
-    keep = 1.0 - shrinkage
-    level = shrinkage * trace_ref[0:1, 0:1] / taps.astype(F32)
-    first_tile = dealt_ref[:, 0:rows, :].reshape(samples, width)
-    panel_ref[:, 0:width] = keep * dot(first_tile, first_tile, ((0,), (0,))) + level * identity(width)
-    panel_ref[:, width:] = jnp.transpose(first_tile.astype(F32))
-    for start in range(0, width, BLOCK):
+def factor_panel(panel_ref, work_ref, order):
+    for start in range(0, order, BLOCK):
         stop = start + BLOCK
         work_ref[:, 0:BLOCK] = panel_ref[start:stop, start:stop]
         work_ref[:, BLOCK:] = identity(BLOCK)
@@ -132,29 +119,60 @@
         panel_ref[start:stop, start:stop] = work_ref[:, 0:BLOCK]
         done = exact_dot(work_ref[:, BLOCK:], panel_ref[start:stop, stop:], ((1,), (0,)))
         panel_ref[start:stop, stop:] = done
-        if stop < width:
-            panel_ref[stop:width, stop:] = panel_ref[stop:width, stop:] - exact_dot(done[:, 0:width - stop], done, ((0,), (0,)))
-    reduced = panel_ref[:, width:]
+        if stop < order:
+            panel_ref[stop:order, stop:] = panel_ref[stop:order, stop:] - exact_dot(done[:, 0:order - stop], done, ((0,), (0,)))
+
+
+def coefficients(place_ref, shrink_ref, trace_ref):
+    shrinkage = shrink_ref[0].astype(F32) / shrink_ref[1].astype(F32)
+    return 1.0 - shrinkage, shrinkage * trace_ref[0:1, 0:1] / place_ref[2].astype(F32)
+
+
+def panel_kernel(place_ref, shrink_ref, trace_ref, scaled_ref, below_ref, diagonal_ref, panel_ref, work_ref):
+    width = scaled_ref.shape[1]
+
+    @pl.when(place_ref[1] == 0)
+    def _():
+        keep, level = coefficients(place_ref, shrink_ref, trace_ref)
+        own = scaled_ref[...]
+        panel_ref[:, 0:width] = (keep / level) * dot(own, own, ((0,), (0,))) + identity(width)
+        panel_ref[:, width:] = jnp.transpose(own.astype(F32))
+        factor_panel(panel_ref, work_ref, width)
+        root = jnp.sqrt(level)
+        below_ref[...] = jnp.transpose(panel_ref[:, width:]) * (keep / root)
+        line = lax.broadcasted_iota(jnp.int32, (width, width), 0)
+        lane = lax.broadcasted_iota(jnp.int32, (width, width), 1)
+        diagonal_ref[...] = jnp.transpose(jnp.where(line <= lane, panel_ref[:, 0:width], 0.0)) * root
+
+
+def tiles_kernel(place_ref, shrink_ref, trace_ref, scaled_ref, below_ref, diagonal_ref, dealt_ref, out_ref, panel_ref, work_ref):
+    sources, _, width = dealt_ref.shape
+    samples = scaled_ref.shape[0]
+    rows = samples // sources
+    positions = out_ref.shape[0]
+    row_index, col_index = place_ref[0], place_ref[1]
+    keep, level = coefficients(place_ref, shrink_ref, trace_ref)
 
     def finish(right):
         right_high, right_low = split(right)
         for position in range(positions):
             tile = dealt_ref[:, (position + 1) * rows:(position + 2) * rows, :].reshape(samples, width)
-            product = dot(tile, right_high, ((0,), (0,))) + dot(tile, right_low, ((0,), (0,)))
-            out_ref[position] = keep * product
+            out_ref[position] = dot(tile, right_high, ((0,), (0,))) + dot(tile, right_low, ((0,), (0,)))
 
     @pl.when(col_index == 0)
     def _():
-        finish(jnp.transpose(reduced))
+        finish(below_ref[...])
 
     @pl.when(col_index > 0)
     def _():
-        high, low = split(reduced)
-        inner = dot(high, high, ((0,), (0,))) + dot(high, low, ((0,), (0,))) + dot(low, high, ((0,), (0,)))
-        inner_high, inner_low = split(inner)
+        first_tile = dealt_ref[:, 0:rows, :].reshape(samples, width)
+        panel_ref[:, 0:samples] = (keep / level) * dot(first_tile, first_tile, ((1,), (1,))) + identity(samples)
+        panel_ref[:, samples:] = identity(samples)
+        factor_panel(panel_ref, work_ref, samples)
+        inverse_factor = panel_ref[:, samples:]
+        high, low = split(keep * exact_dot(inverse_factor, inverse_factor, ((0,), (0,))))
         own = scaled_ref[...]
-        removed = dot(inner_high, own, ((1,), (0,))) + dot(inner_low, own, ((1,), (0,)))
-        finish(own.astype(F32) - keep * removed)
+        finish(dot(high, own, ((1,), (0,))) + dot(low, own, ((1,), (0,))))
         for position in range(positions):
             @pl.when(position * sources + row_index == col_index)
             def _():
@@ -166,10 +184,7 @@
 
     @pl.when((row_index == 0) & (col_index == 0))
     def _():
-        upper = panel_ref[:, 0:width]
-        line = lax.broadcasted_iota(jnp.int32, (width, width), 0)
-        lane = lax.broadcasted_iota(jnp.int32, (width, width), 1)
-        out_ref[0] = jnp.transpose(jnp.where(line <= lane, upper, 0.0))
+        out_ref[0] = diagonal_ref[...]
 
 
 def scale(place, counts, gathered, columns):
@@ -200,20 +215,39 @@
     )(pieces)
 
 
-def factor(place, shrink, trace, scaled, dealt):
+def panel(place, shrink, trace, scaled):
     samples, width = scaled.shape
-    positions = dealt.shape[1] * dealt.shape[0] // samples - 1
-    return pl.pallas_call(
-        factor_kernel,
-        out_shape=jax.ShapeDtypeStruct((positions, width, width), F32),
-        in_specs=[SMEM, SMEM, VMEM, VMEM, VMEM],
-        out_specs=VMEM,
+    return pl.pallas_call(
+        panel_kernel,
+        out_shape=(
+            jax.ShapeDtypeStruct((samples, width), F32),
+            jax.ShapeDtypeStruct((width, width), F32),
+        ),
+        in_specs=[SMEM, SMEM, VMEM, VMEM],
+        out_specs=(VMEM, VMEM),
         scratch_shapes=[
             pltpu.VMEM((width, width + samples), F32),
             pltpu.VMEM((BLOCK, 2 * BLOCK), F32),
         ],
-        compiler_params=pltpu.CompilerParams(vmem_limit_bytes=48 * 2**20),
-    )(place, shrink, trace, scaled, dealt)
+        compiler_params=pltpu.CompilerParams(vmem_limit_bytes=32 * 2**20),
+        cost_estimate=pl.CostEstimate(flops=20 * 10**9, bytes_accessed=2 * 2**20, transcendentals=0),
+    )(place, shrink, trace, scaled)
+
+
+def tiles(place, shrink, trace, scaled, below, diagonal, dealt):
+    samples, width = scaled.shape
+    positions = dealt.shape[1] * dealt.shape[0] // samples - 1
+    return pl.pallas_call(
+        tiles_kernel,
+        out_shape=jax.ShapeDtypeStruct((positions, width, width), F32),
+        in_specs=[SMEM, SMEM] + [VMEM] * 5,
+        out_specs=VMEM,
+        scratch_shapes=[
+            pltpu.VMEM((samples, 2 * samples), F32),
+            pltpu.VMEM((BLOCK, 2 * BLOCK), F32),
+        ],
+        compiler_params=pltpu.CompilerParams(vmem_limit_bytes=32 * 2**20),
+    )(place, shrink, trace, scaled, below, diagonal, dealt)
 
 
 def per_device(samples, counts, shrink_num, shrink_den):
@@ -230,7 +264,8 @@
     exchanged = lax.all_to_all(pieces, "col", 0, 0)
     dealt, trace = deal(exchanged, rows_count)
     dealt = lax.all_to_all(dealt, "row", 0, 0)
-    return factor(place, shrink, trace, scaled, dealt)
+    below, diagonal = panel(place, shrink, trace, scaled)
+    return tiles(place, shrink, trace, scaled, below, diagonal, dealt)
 
 
 def solution(mesh):

time: 112 us -> 103 us (0.920)
  blocking collectives: 30.6 us -> 0 us
  waiting for transfers between devices: 39.3 us -> 57.3 us
  starting transfers between devices: 12.4 us -> 24.4 us
  Pallas kernels: 26.1 us -> 17.1 us
    all_to_all x1 -> x0, blocking collectives: 30.6 us -> none  [per_device(): exchanged = lax.all_to_all(pieces, 'col', 0, 0)]
    all_to_all x0 -> x1, waiting for transfers between devices: none -> 17.4 us  [per_device(): exchanged = lax.all_to_all(pieces, 'col', 0, 0)]
    all_to_all x0 -> x1, starting transfers between devices: none -> 12.1 us  [per_device(): exchanged = lax.all_to_all(pieces, 'col', 0, 0)]
    pallas_call x1 -> x2, Pallas kernels: 24.1 us -> 14.2 us  [the longest x1 13.5 us: tiles(): pl.pallas_call(tiles_kernel, out_shape=jax.ShapeDtypeStruct((positions, w...]
  transfers between devices with their start and end apart: 2 -> 3, of which waited for: 2 -> 3; matrix products, arithmetic and copies ran while one was open for 0% -> 0% of each run, Pallas kernels for 0% -> 1%
where the time goes in v2:
time: 103 us; the launch traced here: 102 us
  waiting for transfers between devices  57.3 us (56%)
  starting transfers between devices  24.4 us (24%)
  Pallas kernels  17.1 us (17%)
  local copies, waits for them, and re-layouts  2.12 us (2%)
  between operations  1.34 us (1%)
    all_to_all x1, waiting for transfers between devices, per_device(): dealt = lax.all_to_all(dealt, 'row', 0, 0)  25.2 us
    all_to_all x1, waiting for transfers between devices, per_device(): exchanged = lax.all_to_all(pieces, 'col', 0, 0)  17.4 us
    all_to_all x1, waiting for transfers between devices, per_device(): gathered = lax.all_to_all(copies, 'row', 0, 0)  14.7 us
    pallas_call x1, Pallas kernels, tiles(): pl.pallas_call(tiles_kernel, out_shape=jax.ShapeDtypeStruct((positions, w...  13.5 us
    all_to_all x1, starting transfers between devices, per_device(): exchanged = lax.all_to_all(pieces, 'col', 0, 0)  12.1 us
    all_to_all x1, starting transfers between devices, per_device(): gathered = lax.all_to_all(copies, 'row', 0, 0)  8.77 us
    all_to_all x1, starting transfers between devices, per_device(): dealt = lax.all_to_all(dealt, 'row', 0, 0)  3.61 us
  transfers between devices with their start and end apart: 3, of which 3 were waited for; matrix products, arithmetic and copies ran while one was open for 0% of the time, Pallas kernels for 1%

profile of v2, /device:TPU:8, one launch (start us, length us, event | category | flops | bytes accessed | tf_op | source)
XLA Modules:
  0.0 102.4 jit_solution(17160051090997171062)
XLA Ops:
  0.0 1.4 %broadcast_in_dim.10 = bf16[16,16,512]{2,1,0:T(8,128)(2,1)} broadcast(bf16[16,512]{1,0:T(8,128)(2,1)} %param.4), dimensions={1,2} | broadcast | bytes 278528 | tf_op jit(solution)/shard_map/broadcast_in_dim | solution.py:261
  1.4 8.8 %all-to-all-start = ((bf16[16,16,512]{2,1,0:T(8,128)(2,1)}), bf16[16,16,512]{2,1,0:T(8,128)(2,1)S(1)}, u32[]{:S(2)}, u32[]{:S(2)}) async-start(bf16[16,16,512]{2,1,0:T(8,128)(2,1)} %broadcast_in_dim.10), calls=%async_computation | async-start | bytes 524288 | tf_op jit(solution)/shard_map/all_to_all | solution.py:262
  10.2 0.1 pad_add_fusion.place_ref
  10.3 14.7 %all-to-all-done.samples_ref = bf16[16,16,512]{2,1,0:T(8,128)(2,1)S(1)} async-done(((bf16[16,16,512]{2,1,0:T(8,128)(2,1)}), bf16[16,16,512]{2,1,0:T(8,128)(2,1)S(1)}, u32[]{:S(2)}, u32[]{:S(2)}) %all-to-all-start) | async-done | bytes 262176 | tf_op jit(solution)/shard_map/all_to_all | solution.py:262
  25.0 0.0 copy-start
  25.0 0.7 copy-done
  25.7 1.9 %shard_map.46 = (bf16[256,512]{1,0:T(8,128)(2,1)S(1)}, bf16[32,16,640]{2,1,0:T(8,128)(2,1)}) custom-call(s32[3]{0:T(128)S(1)} %pad_add_fusion.place_ref, s32[1,256]{1,0:T(1,128)S(1)} %bitcast.3, bf16[16,16,512]{2,1,0:T(8,128)(2,1)S(1)} %all-to-all-done.samples_ref), custom_call_target="tpu_custom_call" | custom-call | tf_op jit(solution)/shard_map/pallas_call | solution.py:192
  27.6 12.1 %all-to-all-start.1 = ((bf16[32,16,640]{2,1,0:T(8,128)(2,1)}), bf16[32,16,640]{2,1,0:T(8,128)(2,1)S(1)}, u32[]{:S(2)}, u32[]{:S(2)}) async-start(bf16[32,16,640]{2,1,0:T(8,128)(2,1)} %get-tuple-element.11), calls=%async_computation.1 | async-start | bytes 1310720 | tf_op jit(solution)/shard_map/all_to_all | solution.py:264
  40.9 0.1 pad_add_fusion.1.shrink_ref
  41.0 17.4 %all-to-all-done.1.pieces_ref = bf16[32,16,640]{2,1,0:T(8,128)(2,1)S(1)} async-done(((bf16[32,16,640]{2,1,0:T(8,128)(2,1)}), bf16[32,16,640]{2,1,0:T(8,128)(2,1)S(1)}, u32[]{:S(2)}, u32[]{:S(2)}) %all-to-all-start.1) | async-done | bytes 655392 | tf_op jit(solution)/shard_map/all_to_all | solution.py:264
  58.4 0.9 shard_map.47
  59.4 3.6 %all-to-all-start.2 = ((bf16[16,48,512]{2,1,0:T(8,128)(2,1)}), bf16[16,48,512]{2,1,0:T(8,128)(2,1)S(1)}, u32[]{:S(2)}, u32[]{:S(2)}) async-start(bf16[16,48,512]{2,1,0:T(8,128)(2,1)} %get-tuple-element.16), calls=%async_computation.2 | async-start | bytes 1572864 | tf_op jit(solution)/shard_map/all_to_all | solution.py:266
  63.0 0.8 shard_map.48
  63.8 25.2 %all-to-all-done.2.dealt_ref = bf16[16,48,512]{2,1,0:T(8,128)(2,1)S(1)} async-done(((bf16[16,48,512]{2,1,0:T(8,128)(2,1)}), bf16[16,48,512]{2,1,0:T(8,128)(2,1)S(1)}, u32[]{:S(2)}, u32[]{:S(2)}) %all-to-all-start.2) | async-done | bytes 786464 | tf_op jit(solution)/shard_map/all_to_all | solution.py:266
  88.9 13.5 %shard_map.49 = f32[2,512,512]{2,1,0:T(8,128)} custom-call(s32[3]{0:T(128)S(1)} %pad_add_fusion.place_ref, s32[2]{0:T(128)S(1)} %pad_add_fusion.1.shrink_ref, f32[8,128]{1,0:T(8,128)S(1)} %get-tuple-element.12.trace_ref, bf16[256,512]{1,0:T(8,128)(2,1)S(1)} %get-tuple-element.13.scaled_ref, f32[256,512]{1,0:T(8,128)S(1)} %get-tuple-element.14.below_ref, ...), custom_call_target="tpu_custom_call" | custom-call | tf_op jit(solution)/shard_map/pallas_call | solution.py:240
Async XLA Ops:
  1.4 23.5 %all-to-all-start = ((bf16[16,16,512]{2,1,0:T(8,128)(2,1)}), bf16[16,16,512]{2,1,0:T(8,128)(2,1)S(1)}, u32[]{:S(2)}, u32[]{:S(2)}) async-start(bf16[16,16,512]{2,1,0:T(8,128)(2,1)} %broadcast_in_dim.10), calls=%async_computation | async-start | bytes 524288 | tf_op jit(solution)/shard_map/all_to_all | solution.py:262
  25.0 0.7 copy-start
  27.6 30.8 %all-to-all-start.1 = ((bf16[32,16,640]{2,1,0:T(8,128)(2,1)}), bf16[32,16,640]{2,1,0:T(8,128)(2,1)S(1)}, u32[]{:S(2)}, u32[]{:S(2)}) async-start(bf16[32,16,640]{2,1,0:T(8,128)(2,1)} %get-tuple-element.11), calls=%async_computation.1 | async-start | bytes 1310720 | tf_op jit(solution)/shard_map/all_to_all | solution.py:264
  59.4 29.6 %all-to-all-start.2 = ((bf16[16,48,512]{2,1,0:T(8,128)(2,1)}), bf16[16,48,512]{2,1,0:T(8,128)(2,1)S(1)}, u32[]{:S(2)}, u32[]{:S(2)}) async-start(bf16[16,48,512]{2,1,0:T(8,128)(2,1)} %get-tuple-element.16), calls=%async_computation.2 | async-start | bytes 1572864 | tf_op jit(solution)/shard_map/all_to_all | solution.py:266

commit v3 on v2

v3 whole, which is shorter than its diff:
```python
import functools

import jax
import jax.numpy as jnp
from jax import lax
from jax.experimental import pallas as pl
from jax.experimental.pallas import tpu as pltpu
from jax.sharding import PartitionSpec as P

BLOCK = 128
MICRO = 32
STRIP = 16
TAIL = 8
F32 = jnp.float32
BF16 = jnp.bfloat16
VMEM = pl.BlockSpec(memory_space=pltpu.VMEM)
SMEM = pl.BlockSpec(memory_space=pltpu.SMEM)


def dot(left, right, dims, precision=None):
    return lax.dot_general(
        left, right, ((dims[0], dims[1]), ((), ())),
        precision=precision, preferred_element_type=F32,
    )


def exact_dot(left, right, dims):
    return dot(left, right, dims, lax.Precision.HIGHEST)


def split(value):
    high = value.astype(BF16)
    return high, (value - high.astype(F32)).astype(BF16)


def copies_kernel(samples_ref, copies_ref):
    for target in range(copies_ref.shape[0]):
        copies_ref[target] = samples_ref[...]


def scale_kernel(counts_ref, samples_ref, scaled_ref, pieces_ref):
    count, rows, width = samples_ref.shape
    number = count * rows
    counts = counts_ref[...].astype(F32)
    weights = jnp.broadcast_to(counts / jnp.sum(counts), (8, number))
    column = jnp.transpose(weights)[:, 0:1]
    values = samples_ref[...].reshape(number, width).astype(F32)
    mean = jnp.sum(column * values, axis=0, keepdims=True)
    scaled = (jnp.sqrt(column) * (values - mean)).astype(BF16)
    scaled_ref[...] = scaled
    share = jnp.sum(jnp.square(scaled.astype(F32)), axis=0, keepdims=True)
    share = jnp.broadcast_to(jnp.sum(share, axis=1, keepdims=True), (TAIL, 128))
    high, middle = split(share)
    low = (share - high.astype(F32) - middle.astype(F32)).astype(BF16)
    line = lax.broadcasted_iota(jnp.int32, (TAIL, 128), 0)
    tail = jnp.where(line == 0, high.astype(F32), 0.0)
    tail = jnp.where(line == 1, middle.astype(F32), tail)
    tail = jnp.where(line == 2, low.astype(F32), tail).astype(BF16)
    first = pl.multiple_of(lax.axis_index("row") * rows, rows)
    own = scaled_ref[pl.ds(first, rows), :]
    body = pieces_ref.shape[1] - TAIL
    for target in range(pieces_ref.shape[0]):
        for part in range(width // 128):
            pieces_ref[target, part * rows:(part + 1) * rows, :] = own[:, part * 128:(part + 1) * 128]
        pieces_ref[target, body:, :] = tail


def deal_kernel(pieces_ref, dealt_ref, trace_ref):
    columns, high, _ = pieces_ref.shape
    targets, dealt_rows, width = dealt_ref.shape
    positions = columns // targets
    rows = dealt_rows // (1 + positions)
    for target in range(targets):
        tiles_of_target = [0] + [position * targets + target for position in range(positions)]
        for place, tile in enumerate(tiles_of_target):
            for part in range(width // 128):
                dealt_ref[target, place * rows:(place + 1) * rows, part * 128:(part + 1) * 128] = pieces_ref[
                    tile, part * rows:(part + 1) * rows, :
                ]
    total = jnp.zeros((TAIL, 128), F32)
    for column in range(columns):
        total = total + pieces_ref[column, high - TAIL:, :].astype(F32)
    trace_ref[...] = jnp.broadcast_to(jnp.sum(total, axis=0, keepdims=True), (8, 128))


def eliminate(work_ref, first, micro):
    lanes = work_ref.shape[1]
    groups = micro // 8
    rows = [[work_ref[first + 8 * g:first + 8 * g + 8, 128 * w:128 * w + 128] for w in range(lanes // 128)] for g in range(groups)]
    part, lane = first // 128, first % 128
    for begin in range(0, micro, STRIP):
        columns = {
            k: {g: jnp.broadcast_to(rows[g][part][:, lane + k:lane + k + 1], (8, 128)) for g in range(begin // 8, groups)}
            for k in range(begin, begin + STRIP)
        }
        for j in range(begin, begin + STRIP):
            group, line = j // 8, j % 8

            def spread(value):
                return jnp.broadcast_to(value[line:line + 1, :], (8, 128))

            pivot = spread(columns[j][group])
            inverse = 1.0 / pivot
            scale = lax.rsqrt(pivot)
            live = range((j + 1) // 8, groups)
            multiplier = {g: columns[j][g] * inverse for g in live}
            for k in range(j + 1, begin + STRIP):
                entry = spread(columns[k][group])
                for g in live:
                    columns[k][g] = columns[k][g] - multiplier[g] * entry
            for w in range(lanes // 128):
                entry = spread(rows[group][w])
                work_ref[first + j:first + j + 1, 128 * w:128 * w + 128] = (entry * scale)[0:1, :]
                for g in live:
                    rows[g][w] = rows[g][w] - multiplier[g] * entry


def factor_block(work_ref, block, micro):
    for first in range(0, block, micro):
        eliminate(work_ref, first, micro)
        after = first + micro
        if after < block:
            panel = work_ref[first:after, :]
            work_ref[after:, :] = work_ref[after:, :] - exact_dot(panel[:, after:block], panel, ((0,), (0,)))


def identity(size):
    return jnp.where(
        lax.broadcasted_iota(jnp.int32, (size, size), 0) == lax.broadcasted_iota(jnp.int32, (size, size), 1), 1.0, 0.0
    ).astype(F32)


def factor_panel(panel_ref, work_ref, order):
    for start in range(0, order, BLOCK):
        stop = start + BLOCK
        work_ref[:, 0:BLOCK] = panel_ref[start:stop, start:stop]
        work_ref[:, BLOCK:] = identity(BLOCK)
        factor_block(work_ref, BLOCK, MICRO)
        panel_ref[start:stop, start:stop] = work_ref[:, 0:BLOCK]
        done = exact_dot(work_ref[:, BLOCK:], panel_ref[start:stop, stop:], ((1,), (0,)))
        panel_ref[start:stop, stop:] = done
        if stop < order:
            panel_ref[stop:order, stop:] = panel_ref[stop:order, stop:] - exact_dot(done[:, 0:order - stop], done, ((0,), (0,)))


def coefficients(number_ref, over_ref, trace_ref, taps):
    shrinkage = number_ref[0].astype(F32) / over_ref[0].astype(F32)
    return 1.0 - shrinkage, shrinkage * trace_ref[0:1, 0:1] / taps


def panel_kernel(taps, number_ref, over_ref, trace_ref, scaled_ref, below_ref, diagonal_ref, panel_ref, work_ref):
    width = scaled_ref.shape[1]

    @pl.when(lax.axis_index("col") == 0)
    def _():
        keep, level = coefficients(number_ref, over_ref, trace_ref, taps)
        own = scaled_ref[...]
        panel_ref[:, 0:width] = (keep / level) * dot(own, own, ((0,), (0,))) + identity(width)
        panel_ref[:, width:] = jnp.transpose(own.astype(F32))
        factor_panel(panel_ref, work_ref, width)
        root = jnp.sqrt(level)
        below_ref[...] = jnp.transpose(panel_ref[:, width:]) * (keep / root)
        line = lax.broadcasted_iota(jnp.int32, (width, width), 0)
        lane = lax.broadcasted_iota(jnp.int32, (width, width), 1)
        diagonal_ref[...] = jnp.transpose(jnp.where(line <= lane, panel_ref[:, 0:width], 0.0)) * root


def tiles_kernel(taps, number_ref, over_ref, trace_ref, scaled_ref, below_ref, diagonal_ref, dealt_ref, out_ref, panel_ref, work_ref):
    sources, _, width = dealt_ref.shape
    samples = scaled_ref.shape[0]
    rows = samples // sources
    positions = out_ref.shape[0]
    row_index, col_index = lax.axis_index("row"), lax.axis_index("col")
    keep, level = coefficients(number_ref, over_ref, trace_ref, taps)

    def finish(right):
        right_high, right_low = split(right)
        for position in range(positions):
            tile = dealt_ref[:, (position + 1) * rows:(position + 2) * rows, :].reshape(samples, width)
            out_ref[position] = dot(tile, right_high, ((0,), (0,))) + dot(tile, right_low, ((0,), (0,)))

    @pl.when(col_index == 0)
    def _():
        finish(below_ref[...])

    @pl.when(col_index > 0)
    def _():
        first_tile = dealt_ref[:, 0:rows, :].reshape(samples, width)
        panel_ref[:, 0:samples] = (keep / level) * dot(first_tile, first_tile, ((1,), (1,))) + identity(samples)
        panel_ref[:, samples:] = identity(samples)
        factor_panel(panel_ref, work_ref, samples)
        inverse_factor = panel_ref[:, samples:]
        high, low = split(keep * exact_dot(inverse_factor, inverse_factor, ((0,), (0,))))
        own = scaled_ref[...]
        finish(dot(high, own, ((1,), (0,))) + dot(low, own, ((1,), (0,))))
        for position in range(positions):
            @pl.when(position * sources + row_index == col_index)
            def _():
                out_ref[position] = out_ref[position] + level * identity(width)

    @pl.when((row_index == 0) & (col_index > 0))
    def _():
        out_ref[0] = jnp.zeros((width, width), F32)

    @pl.when((row_index == 0) & (col_index == 0))
    def _():
        out_ref[0] = diagonal_ref[...]


def limit(mebibytes):
    return pltpu.CompilerParams(vmem_limit_bytes=mebibytes * 2**20)


def copies(samples, count):
    return pl.pallas_call(
        copies_kernel,
        out_shape=jax.ShapeDtypeStruct((count, *samples.shape), BF16),
        in_specs=[VMEM],
        out_specs=VMEM,
        compiler_params=limit(8),
    )(samples)


def scale(counts, gathered, columns):
    count, rows, width = gathered.shape
    return pl.pallas_call(
        scale_kernel,
        out_shape=(
            jax.ShapeDtypeStruct((count * rows, width), BF16),
            jax.ShapeDtypeStruct((columns, rows * width // 128 + TAIL, 128), BF16),
        ),
        in_specs=[VMEM, VMEM],
        out_specs=(VMEM, VMEM),
        compiler_params=limit(16),
    )(counts[None, :], gathered)


def deal(pieces, rows, width, targets):
    columns = pieces.shape[0]
    return pl.pallas_call(
        deal_kernel,
        out_shape=(
            jax.ShapeDtypeStruct((targets, (1 + columns // targets) * rows, width), BF16),
            jax.ShapeDtypeStruct((8, 128), F32),
        ),
        in_specs=[VMEM],
        out_specs=(VMEM, VMEM),
        compiler_params=limit(16),
    )(pieces)


def panel(number, over, trace, scaled, taps):
    samples, width = scaled.shape
    return pl.pallas_call(
        functools.partial(panel_kernel, taps),
        out_shape=(
            jax.ShapeDtypeStruct((samples, width), F32),
            jax.ShapeDtypeStruct((width, width), F32),
        ),
        in_specs=[SMEM, SMEM, VMEM, VMEM],
        out_specs=(VMEM, VMEM),
        scratch_shapes=[
            pltpu.VMEM((width, width + samples), F32),
            pltpu.VMEM((BLOCK, 2 * BLOCK), F32),
        ],
        compiler_params=limit(32),
        cost_estimate=pl.CostEstimate(flops=20 * 10**9, bytes_accessed=2 * 2**20, transcendentals=0),
    )(number, over, trace, scaled)


def tiles(number, over, trace, scaled, below, diagonal, dealt, taps):
    samples, width = scaled.shape
    positions = dealt.shape[1] * dealt.shape[0] // samples - 1
    return pl.pallas_call(
        functools.partial(tiles_kernel, taps),
        out_shape=jax.ShapeDtypeStruct((positions, width, width), F32),
        in_specs=[SMEM, SMEM] + [VMEM] * 5,
        out_specs=VMEM,
        scratch_shapes=[
            pltpu.VMEM((samples, 2 * samples), F32),
            pltpu.VMEM((BLOCK, 2 * BLOCK), F32),
        ],
        compiler_params=limit(32),
    )(number, over, trace, scaled, below, diagonal, dealt)


def per_device(samples, counts, shrink_num, shrink_den):
    rows_count = lax.axis_size("row")
    cols_count = lax.axis_size("col")
    rows, width = samples.shape
    taps = width * cols_count
    gathered = lax.all_to_all(copies(samples, rows_count), "row", 0, 0)
    scaled, pieces = scale(counts, gathered, cols_count)
    exchanged = lax.all_to_all(pieces, "col", 0, 0)
    dealt, trace = deal(exchanged, rows, width, rows_count)
    dealt = lax.all_to_all(dealt, "row", 0, 0)
    below, diagonal = panel(shrink_num, shrink_den, trace, scaled, taps)
    return tiles(shrink_num, shrink_den, trace, scaled, below, diagonal, dealt, taps)


def solution(mesh):
    in_specs = (P("row", "col"), P(), P(), P())
    out_specs = P(None, "row", "col")
    return jax.shard_map(
        per_device, mesh=mesh, in_specs=in_specs, out_specs=out_specs, check_vma=False
    )
```

time: 103 us -> 98 us (0.951)
  the two profiles are of different devices: /device:TPU:8 before, /device:TPU:16 now
where the time goes in v3:
time: 98 us; the launch traced here: 97.6 us
  waiting for transfers between devices  42.1 us (43%)
  blocking collectives  22.4 us (23%)
  starting transfers between devices  16.4 us (17%)
  Pallas kernels  14 us (14%)
  local copies, waits for them, and re-layouts  1.4 us (1%)
  between operations  1.33 us (1%)
    all_to_all x1, waiting for transfers between devices, per_device(): dealt = lax.all_to_all(dealt, 'row', 0, 0)  25.9 us
    all_to_all x1, blocking collectives, per_device(): gathered = lax.all_to_all(copies(samples, rows_count), 'row', 0, 0)  22.4 us
    all_to_all x1, waiting for transfers between devices, per_device(): exchanged = lax.all_to_all(pieces, 'col', 0, 0)  16.2 us
    all_to_all x1, starting transfers between devices, per_device(): exchanged = lax.all_to_all(pieces, 'col', 0, 0)  12.8 us
    pallas_call x1, Pallas kernels, tiles(): pl.pallas_call(functools.partial(tiles_kernel, taps), out_shape=jax.Shape...  11.6 us
    all_to_all x1, starting transfers between devices, per_device(): dealt = lax.all_to_all(dealt, 'row', 0, 0)  3.61 us
  transfers between devices with their start and end apart: 2, of which 2 were waited for; matrix products, arithmetic and copies ran while one was open for 0% of the time, Pallas kernels for 0%

profile of v3, /device:TPU:16, one launch (start us, length us, event | category | flops | bytes accessed | tf_op | source)
XLA Modules:
  0.0 97.6 jit_solution(6556313800838000742)
XLA Ops:
  0.0 0.0 copy-start
  0.0 0.7 copy-done
  0.7 22.4 %all_to_all.15.samples_ref = bf16[16,16,512]{2,1,0:T(8,128)(2,1)S(1)} all-to-all(bf16[16,16,512]{2,1,0:T(8,128)(2,1)S(1)} %shard_map.46), channel_id=1, replica_groups=mesh['row'=16,'col'=32] {'row'}, dimensions={0} | all-to-all | bytes 524288 | tf_op jit(solution)/shard_map/all_to_all | solution.py:292
  23.2 0.0 copy-start.1
  23.2 0.7 copy-done.1
  23.9 1.4 %shard_map.47 = (bf16[256,512]{1,0:T(8,128)(2,1)S(1)}, bf16[32,72,128]{2,1,0:T(8,128)(2,1)}) custom-call(s32[1,256]{1,0:T(1,128)S(1)} %bitcast.1, bf16[16,16,512]{2,1,0:T(8,128)(2,1)S(1)} %all_to_all.15.samples_ref), custom_call_target="tpu_custom_call" | custom-call | tf_op jit(solution)/shard_map/pallas_call | solution.py:226
  25.2 12.8 %all-to-all-start.1 = ((bf16[32,72,128]{2,1,0:T(8,128)(2,1)}), bf16[32,72,128]{2,1,0:T(8,128)(2,1)S(1)}, u32[]{:S(2)}, u32[]{:S(2)}) async-start(bf16[32,72,128]{2,1,0:T(8,128)(2,1)} %get-tuple-element.11), calls=%async_computation.1 | async-start | bytes 1179648 | tf_op jit(solution)/shard_map/all_to_all | solution.py:294
  39.4 16.2 %all-to-all-done.1.pieces_ref = bf16[32,72,128]{2,1,0:T(8,128)(2,1)S(1)} async-done(((bf16[32,72,128]{2,1,0:T(8,128)(2,1)}), bf16[32,72,128]{2,1,0:T(8,128)(2,1)S(1)}, u32[]{:S(2)}, u32[]{:S(2)}) %all-to-all-start.1) | async-done | bytes 589856 | tf_op jit(solution)/shard_map/all_to_all | solution.py:294
  55.5 1.0 %shard_map.48 = (bf16[16,48,512]{2,1,0:T(8,128)(2,1)}, f32[8,128]{1,0:T(8,128)S(1)}) custom-call(bf16[32,72,128]{2,1,0:T(8,128)(2,1)S(1)} %all-to-all-done.1.pieces_ref), custom_call_target="tpu_custom_call" | custom-call | tf_op jit(solution)/shard_map/pallas_call | solution.py:240
  56.5 3.6 %all-to-all-start.2 = ((bf16[16,48,512]{2,1,0:T(8,128)(2,1)}), bf16[16,48,512]{2,1,0:T(8,128)(2,1)S(1)}, u32[]{:S(2)}, u32[]{:S(2)}) async-start(bf16[16,48,512]{2,1,0:T(8,128)(2,1)} %get-tuple-element.16), calls=%async_computation.2 | async-start | bytes 1572864 | tf_op jit(solution)/shard_map/all_to_all | solution.py:296
  60.2 25.9 %all-to-all-done.2.dealt_ref = bf16[16,48,512]{2,1,0:T(8,128)(2,1)S(1)} async-done(((bf16[16,48,512]{2,1,0:T(8,128)(2,1)}), bf16[16,48,512]{2,1,0:T(8,128)(2,1)S(1)}, u32[]{:S(2)}, u32[]{:S(2)}) %all-to-all-start.2) | async-done | bytes 786464 | tf_op jit(solution)/shard_map/all_to_all | solution.py:296
  86.0 11.6 %shard_map.50 = f32[2,512,512]{2,1,0:T(8,128)} custom-call(s32[1]{0:T(128)S(6)} %copy.5.number_ref, s32[1]{0:T(128)S(6)} %copy.6.over_ref, f32[8,128]{1,0:T(8,128)S(1)} %get-tuple-element.12.trace_ref, bf16[256,512]{1,0:T(8,128)(2,1)S(1)} %get-tuple-element.13.scaled_ref, f32[256,512]{1,0:T(8,128)S(1)} %get-tuple-element.14.below_ref, ...), custom_call_target="tpu_custom_call" | custom-call | tf_op jit(solution)/shard_map/pallas_call | solution.py:274
  (2 shorter events, 0.0 us)
Async XLA Ops:
  0.0 0.7 copy-start
  23.2 0.7 copy-start.1
  25.2 30.3 %all-to-all-start.1 = ((bf16[32,72,128]{2,1,0:T(8,128)(2,1)}), bf16[32,72,128]{2,1,0:T(8,128)(2,1)S(1)}, u32[]{:S(2)}, u32[]{:S(2)}) async-start(bf16[32,72,128]{2,1,0:T(8,128)(2,1)} %get-tuple-element.11), calls=%async_computation.1 | async-start | bytes 1179648 | tf_op jit(solution)/shard_map/all_to_all | solution.py:294
  56.5 29.5 %all-to-all-start.2 = ((bf16[16,48,512]{2,1,0:T(8,128)(2,1)}), bf16[16,48,512]{2,1,0:T(8,128)(2,1)S(1)}, u32[]{:S(2)}, u32[]{:S(2)}) async-start(bf16[16,48,512]{2,1,0:T(8,128)(2,1)} %get-tuple-element.16), calls=%async_computation.2 | async-start | bytes 1572864 | tf_op jit(solution)/shard_map/all_to_all | solution.py:296

commit v4 on v3

--- a/solution.py
+++ b/solution.py
@@ -11,6 +11,7 @@
 MICRO = 32
 STRIP = 16
 TAIL = 8
+COARSE = 4
 F32 = jnp.float32
 BF16 = jnp.bfloat16
 VMEM = pl.BlockSpec(memory_space=pltpu.VMEM)
@@ -24,16 +25,37 @@
     )
 
 
-def exact_dot(left, right, dims):
-    return dot(left, right, dims, lax.Precision.HIGHEST)
-
-
 def split(value):
     high = value.astype(BF16)
     return high, (value - high.astype(F32)).astype(BF16)
 
 
-def copies_kernel(samples_ref, copies_ref):
+def thirds(value):
+    high, rest = value.astype(BF16), value
+    rest = rest - high.astype(F32)
+    middle = rest.astype(BF16)
+    return high, middle, (rest - middle.astype(F32)).astype(BF16)
+
+
+def stack(parts, order, axis):
+    return jnp.concatenate([parts[which] for which in order], axis=axis)
+
+
+LEFT, RIGHT = (0, 0, 1, 0, 1, 2), (0, 1, 0, 2, 1, 0)
+
+
+def gram(value, first, last):
+    parts = thirds(value)
+    left = stack([part[:, first:last] for part in parts], LEFT, 0)
+    return dot(left, stack(parts, RIGHT, 0), ((0,), (0,)))
+
+
+def product(left, right):
+    return dot(stack(thirds(left), LEFT, 1), stack(thirds(right), RIGHT, 0), ((1,), (0,)))
+
+
+def copies_kernel(counts_ref, samples_ref, copies_ref, held_ref):
+    held_ref[...] = counts_ref[...]
     for target in range(copies_ref.shape[0]):
         copies_ref[target] = samples_ref[...]
 
@@ -121,7 +143,7 @@
         after = first + micro
         if after < block:
             panel = work_ref[first:after, :]
-            work_ref[after:, :] = work_ref[after:, :] - exact_dot(panel[:, after:block], panel, ((0,), (0,)))
+            work_ref[after:, :] = work_ref[after:, :] - gram(panel, after, block)
 
 
 def identity(size):
@@ -137,10 +159,10 @@
         work_ref[:, BLOCK:] = identity(BLOCK)
         factor_block(work_ref, BLOCK, MICRO)
         panel_ref[start:stop, start:stop] = work_ref[:, 0:BLOCK]
-        done = exact_dot(work_ref[:, BLOCK:], panel_ref[start:stop, stop:], ((1,), (0,)))
+        done = product(work_ref[:, BLOCK:], panel_ref[start:stop, stop:])
         panel_ref[start:stop, stop:] = done
         if stop < order:
-            panel_ref[stop:order, stop:] = panel_ref[stop:order, stop:] - exact_dot(done[:, 0:order - stop], done, ((0,), (0,)))
+            panel_ref[stop:order, stop:] = panel_ref[stop:order, stop:] - gram(done, 0, order - stop)
 
 
 def coefficients(number_ref, over_ref, trace_ref, taps):
@@ -174,10 +196,10 @@
     keep, level = coefficients(number_ref, over_ref, trace_ref, taps)
 
     def finish(right):
-        right_high, right_low = split(right)
+        both = jnp.concatenate(split(right), axis=0)
         for position in range(positions):
             tile = dealt_ref[:, (position + 1) * rows:(position + 2) * rows, :].reshape(samples, width)
-            out_ref[position] = dot(tile, right_high, ((0,), (0,))) + dot(tile, right_low, ((0,), (0,)))
+            out_ref[position] = dot(jnp.concatenate([tile, tile], axis=0), both, ((0,), (0,)))
 
     @pl.when(col_index == 0)
     def _():
@@ -190,9 +212,9 @@
         panel_ref[:, samples:] = identity(samples)
         factor_panel(panel_ref, work_ref, samples)
         inverse_factor = panel_ref[:, samples:]
-        high, low = split(keep * exact_dot(inverse_factor, inverse_factor, ((0,), (0,))))
+        parts = jnp.concatenate(split(keep * gram(inverse_factor, 0, samples)), axis=1)
         own = scaled_ref[...]
-        finish(dot(high, own, ((1,), (0,))) + dot(low, own, ((1,), (0,))))
+        finish(dot(parts, jnp.concatenate([own, own], axis=0), ((1,), (0,))))
         for position in range(positions):
             @pl.when(position * sources + row_index == col_index)
             def _():
@@ -211,14 +233,17 @@
     return pltpu.CompilerParams(vmem_limit_bytes=mebibytes * 2**20)
 
 
-def copies(samples, count):
+def copies(counts, samples, count):
     return pl.pallas_call(
         copies_kernel,
-        out_shape=jax.ShapeDtypeStruct((count, *samples.shape), BF16),
-        in_specs=[VMEM],
-        out_specs=VMEM,
+        out_shape=(
+            jax.ShapeDtypeStruct((count, *samples.shape), BF16),
+            jax.ShapeDtypeStruct((1, *counts.shape), counts.dtype),
+        ),
+        in_specs=[VMEM, VMEM],
+        out_specs=(VMEM, VMEM),
         compiler_params=limit(8),
-    )(samples)
+    )(counts[None, :], samples)
 
 
 def scale(counts, gathered, columns):
@@ -232,7 +257,7 @@
         in_specs=[VMEM, VMEM],
         out_specs=(VMEM, VMEM),
         compiler_params=limit(16),
-    )(counts[None, :], gathered)
+    )(counts, gathered)
 
 
 def deal(pieces, rows, width, targets):
@@ -284,16 +309,28 @@
     )(number, over, trace, scaled, below, diagonal, dealt)
 
 
+def near_groups(rows_count, cols_count):
+    fine = cols_count // COARSE
+    groups = []
+    for column in range(cols_count):
+        mirrored = (COARSE - 1 - column // fine) * fine + column % fine
+        groups.append(
+            [row * cols_count + (column if 2 * row < rows_count else mirrored) for row in range(rows_count)]
+        )
+    return groups
+
+
 def per_device(samples, counts, shrink_num, shrink_den):
     rows_count = lax.axis_size("row")
     cols_count = lax.axis_size("col")
     rows, width = samples.shape
     taps = width * cols_count
-    gathered = lax.all_to_all(copies(samples, rows_count), "row", 0, 0)
+    own, counts = copies(counts, samples, rows_count)
+    gathered = lax.all_to_all(own, "row", 0, 0)
     scaled, pieces = scale(counts, gathered, cols_count)
     exchanged = lax.all_to_all(pieces, "col", 0, 0)
     dealt, trace = deal(exchanged, rows, width, rows_count)
-    dealt = lax.all_to_all(dealt, "row", 0, 0)
+    dealt = lax.all_to_all(dealt, ("row", "col"), 0, 0, axis_index_groups=near_groups(rows_count, cols_count))
     below, diagonal = panel(shrink_num, shrink_den, trace, scaled, taps)
     return tiles(shrink_num, shrink_den, trace, scaled, below, diagonal, dealt, taps)
 

time: 98 us -> 94.2 us (0.961)
  the two profiles are of different devices: /device:TPU:16 before, /device:TPU:64 now
where the time goes in v4:
time: 94.2 us; the launch traced here: 93.8 us
  waiting for transfers between devices  40.4 us (43%)
  blocking collectives  21.5 us (23%)
  starting transfers between devices  16.7 us (18%)
  Pallas kernels  12.5 us (13%)
  local copies, waits for them, and re-layouts  1.4 us (1%)
  between operations  1.33 us (1%)
    all_to_all x1, waiting for transfers between devices, per_device(): lax.all_to_all(dealt, ('row', 'col'), 0, 0, axis_index_groups=near_groups...  23.2 us
    all_to_all x1, blocking collectives, per_device(): gathered = lax.all_to_all(own, 'row', 0, 0)  21.5 us
    all_to_all x1, waiting for transfers between devices, per_device(): exchanged = lax.all_to_all(pieces, 'col', 0, 0)  17.1 us
    all_to_all x1, starting transfers between devices, per_device(): exchanged = lax.all_to_all(pieces, 'col', 0, 0)  13.1 us
    pallas_call x1, Pallas kernels, tiles(): pl.pallas_call(functools.partial(tiles_kernel, taps), out_shape=jax.Shape...  10.1 us
    all_to_all x1, starting transfers between devices, per_device(): lax.all_to_all(dealt, ('row', 'col'), 0, 0, axis_index_groups=near_groups...  3.61 us
  transfers between devices with their start and end apart: 2, of which 2 were waited for; matrix products, arithmetic and copies ran while one was open for 0% of the time, Pallas kernels for 0%

profile of v4, /device:TPU:64, one launch (start us, length us, event | category | flops | bytes accessed | tf_op | source)
XLA Modules:
  0.0 93.8 jit_solution(2728961486171928344)
XLA Ops:
  0.0 0.0 copy-start
  0.0 0.7 copy-done
  0.7 0.0 copy-start.1
  0.7 0.7 copy-done.1
  1.4 21.5 %all_to_all.15.samples_ref = bf16[16,16,512]{2,1,0:T(8,128)(2,1)S(1)} all-to-all(bf16[16,16,512]{2,1,0:T(8,128)(2,1)S(1)} %get-tuple-element.14), channel_id=1, replica_groups=mesh['row'=16,'col'=32] {'row'}, dimensions={0} | all-to-all | bytes 524288 | tf_op jit(solution)/shard_map/all_to_all | solution.py:329
  22.9 1.4 %shard_map.47 = (bf16[256,512]{1,0:T(8,128)(2,1)S(1)}, bf16[32,72,128]{2,1,0:T(8,128)(2,1)}) custom-call(s32[1,256]{1,0:T(1,128)S(1)} %get-tuple-element.13.counts_ref, bf16[16,16,512]{2,1,0:T(8,128)(2,1)S(1)} %all_to_all.15.samples_ref), custom_call_target="tpu_custom_call" | custom-call | tf_op jit(solution)/shard_map/pallas_call | solution.py:251
  24.3 13.1 %all-to-all-start.1 = ((bf16[32,72,128]{2,1,0:T(8,128)(2,1)}), bf16[32,72,128]{2,1,0:T(8,128)(2,1)S(1)}, u32[]{:S(2)}, u32[]{:S(2)}) async-start(bf16[32,72,128]{2,1,0:T(8,128)(2,1)} %get-tuple-element.15), calls=%async_computation.1 | async-start | bytes 1179648 | tf_op jit(solution)/shard_map/all_to_all | solution.py:331
  38.7 17.1 %all-to-all-done.1.pieces_ref = bf16[32,72,128]{2,1,0:T(8,128)(2,1)S(1)} async-done(((bf16[32,72,128]{2,1,0:T(8,128)(2,1)}), bf16[32,72,128]{2,1,0:T(8,128)(2,1)S(1)}, u32[]{:S(2)}, u32[]{:S(2)}) %all-to-all-start.1) | async-done | bytes 589856 | tf_op jit(solution)/shard_map/all_to_all | solution.py:331
  55.8 1.0 %shard_map.48 = (bf16[16,48,512]{2,1,0:T(8,128)(2,1)}, f32[8,128]{1,0:T(8,128)S(1)}) custom-call(bf16[32,72,128]{2,1,0:T(8,128)(2,1)S(1)} %all-to-all-done.1.pieces_ref), custom_call_target="tpu_custom_call" | custom-call | tf_op jit(solution)/shard_map/pallas_call | solution.py:265
  56.8 3.6 %all-to-all-start.2 = ((bf16[16,48,512]{2,1,0:T(8,128)(2,1)}), bf16[16,48,512]{2,1,0:T(8,128)(2,1)S(1)}, u32[]{:S(2)}, u32[]{:S(2)}) async-start(bf16[16,48,512]{2,1,0:T(8,128)(2,1)} %get-tuple-element.20), calls=%async_computation.2 | async-start | bytes 1572864 | tf_op jit(solution)/shard_map/all_to_all | solution.py:333
  60.4 23.2 %all-to-all-done.2.dealt_ref = bf16[16,48,512]{2,1,0:T(8,128)(2,1)S(1)} async-done(((bf16[16,48,512]{2,1,0:T(8,128)(2,1)}), bf16[16,48,512]{2,1,0:T(8,128)(2,1)S(1)}, u32[]{:S(2)}, u32[]{:S(2)}) %all-to-all-start.2) | async-done | bytes 786464 | tf_op jit(solution)/shard_map/all_to_all | solution.py:333
  83.7 10.1 %shard_map.50 = f32[2,512,512]{2,1,0:T(8,128)} custom-call(s32[1]{0:T(128)S(6)} %copy.5.number_ref, s32[1]{0:T(128)S(6)} %copy.6.over_ref, f32[8,128]{1,0:T(8,128)S(1)} %get-tuple-element.16.trace_ref, bf16[256,512]{1,0:T(8,128)(2,1)S(1)} %get-tuple-element.17.scaled_ref, f32[256,512]{1,0:T(8,128)S(1)} %get-tuple-element.18.below_ref, ...), custom_call_target="tpu_custom_call" | custom-call | tf_op jit(solution)/shard_map/pallas_call | solution.py:299
  (2 shorter events, 0.0 us)
Async XLA Ops:
  0.0 0.7 copy-start
  0.7 0.7 copy-start.1
  24.3 31.5 %all-to-all-start.1 = ((bf16[32,72,128]{2,1,0:T(8,128)(2,1)}), bf16[32,72,128]{2,1,0:T(8,128)(2,1)S(1)}, u32[]{:S(2)}, u32[]{:S(2)}) async-start(bf16[32,72,128]{2,1,0:T(8,128)(2,1)} %get-tuple-element.15), calls=%async_computation.1 | async-start | bytes 1179648 | tf_op jit(solution)/shard_map/all_to_all | solution.py:331
  56.8 26.9 %all-to-all-start.2 = ((bf16[16,48,512]{2,1,0:T(8,128)(2,1)}), bf16[16,48,512]{2,1,0:T(8,128)(2,1)S(1)}, u32[]{:S(2)}, u32[]{:S(2)}) async-start(bf16[16,48,512]{2,1,0:T(8,128)(2,1)} %get-tuple-element.20), calls=%async_computation.2 | async-start | bytes 1572864 | tf_op jit(solution)/shard_map/all_to_all | solution.py:333

commit v5 on v4

--- a/solution.py
+++ b/solution.py
@@ -60,15 +60,23 @@
         copies_ref[target] = samples_ref[...]
 
 
-def scale_kernel(counts_ref, samples_ref, scaled_ref, pieces_ref):
+def columns_of(counts):
+    counts = counts.astype(F32)
+    weights = jnp.broadcast_to(counts / jnp.sum(counts), (128, counts.shape[1]))
+    return jnp.transpose(weights)
+
+
+def scale_tile(weights, roots, samples):
+    repeats = samples.shape[1] // 128
+    values = samples.astype(F32)
+    mean = jnp.sum(jnp.concatenate([weights] * repeats, axis=1) * values, axis=0, keepdims=True)
+    return (jnp.concatenate([roots] * repeats, axis=1) * (values - mean)).astype(BF16)
+
+
+def scale_kernel(counts_ref, samples_ref, helped_ref, helped_too_ref, scaled_ref, pieces_ref):
     count, rows, width = samples_ref.shape
-    number = count * rows
-    counts = counts_ref[...].astype(F32)
-    weights = jnp.broadcast_to(counts / jnp.sum(counts), (8, number))
-    column = jnp.transpose(weights)[:, 0:1]
-    values = samples_ref[...].reshape(number, width).astype(F32)
-    mean = jnp.sum(column * values, axis=0, keepdims=True)
-    scaled = (jnp.sqrt(column) * (values - mean)).astype(BF16)
+    weights = columns_of(counts_ref[...])
+    scaled = scale_tile(weights, jnp.sqrt(weights), samples_ref[...].reshape(count * rows, width))
     scaled_ref[...] = scaled
     share = jnp.sum(jnp.square(scaled.astype(F32)), axis=0, keepdims=True)
     share = jnp.broadcast_to(jnp.sum(share, axis=1, keepdims=True), (TAIL, 128))
@@ -78,26 +86,33 @@
     tail = jnp.where(line == 0, high.astype(F32), 0.0)
     tail = jnp.where(line == 1, middle.astype(F32), tail)
     tail = jnp.where(line == 2, low.astype(F32), tail).astype(BF16)
-    first = pl.multiple_of(lax.axis_index("row") * rows, rows)
-    own = scaled_ref[pl.ds(first, rows), :]
+    half, place = lax.axis_index("row") // (count // 2), lax.rem(lax.axis_index("row"), count // 2)
+    column = lax.axis_index("col")
+    fine = pieces_ref.shape[0] // COARSE
+    own = lax.rem(column // fine, 2) == half
+    own = (column == 0) | (own & ((half == 0) | (column != fine)))
+    helped = helped_ref[...].astype(F32) + helped_too_ref[...].astype(F32)
+    sent = jnp.where(own, samples_ref[2 * place].astype(F32), helped).astype(BF16)
     body = pieces_ref.shape[1] - TAIL
     for target in range(pieces_ref.shape[0]):
         for part in range(width // 128):
-            pieces_ref[target, part * rows:(part + 1) * rows, :] = own[:, part * 128:(part + 1) * 128]
+            pieces_ref[target, part * rows:(part + 1) * rows, :] = sent[:, part * 128:(part + 1) * 128]
         pieces_ref[target, body:, :] = tail
 
 
 def deal_kernel(pieces_ref, dealt_ref, trace_ref):
     columns, high, _ = pieces_ref.shape
     targets, dealt_rows, width = dealt_ref.shape
-    positions = columns // targets
-    rows = dealt_rows // (1 + positions)
+    fine = columns // COARSE
+    rows = dealt_rows // 6
+    half = lax.axis_index("row") // targets
+    first, second = half * fine, (1 - half) * fine
     for target in range(targets):
-        tiles_of_target = [0] + [position * targets + target for position in range(positions)]
-        for place, tile in enumerate(tiles_of_target):
+        sources = (0, fine, first + target, second + target, first + 2 * fine + target, second + 2 * fine + target)
+        for place, source in enumerate(sources):
             for part in range(width // 128):
                 dealt_ref[target, place * rows:(place + 1) * rows, part * 128:(part + 1) * 128] = pieces_ref[
-                    tile, part * rows:(part + 1) * rows, :
+                    source, part * rows:(part + 1) * rows, :
                 ]
     total = jnp.zeros((TAIL, 128), F32)
     for column in range(columns):
@@ -187,38 +202,68 @@
         diagonal_ref[...] = jnp.transpose(jnp.where(line <= lane, panel_ref[:, 0:width], 0.0)) * root
 
 
-def tiles_kernel(taps, number_ref, over_ref, trace_ref, scaled_ref, below_ref, diagonal_ref, dealt_ref, out_ref, panel_ref, work_ref):
-    sources, _, width = dealt_ref.shape
-    samples = scaled_ref.shape[0]
-    rows = samples // sources
-    positions = out_ref.shape[0]
-    row_index, col_index = lax.axis_index("row"), lax.axis_index("col")
-    keep, level = coefficients(number_ref, over_ref, trace_ref, taps)
-
-    def finish(right):
-        both = jnp.concatenate(split(right), axis=0)
-        for position in range(positions):
-            tile = dealt_ref[:, (position + 1) * rows:(position + 2) * rows, :].reshape(samples, width)
-            out_ref[position] = dot(jnp.concatenate([tile, tile], axis=0), both, ((0,), (0,)))
-
-    @pl.when(col_index == 0)
-    def _():
-        finish(below_ref[...])
-
-    @pl.when(col_index > 0)
-    def _():
-        first_tile = dealt_ref[:, 0:rows, :].reshape(samples, width)
+def right_kernel(
+    taps, number_ref, over_ref, trace_ref, counts_ref, scaled_ref, below_ref, dealt_ref, right_ref, tiles_ref, panel_ref, work_ref
+):
+    samples, width = scaled_ref.shape
+    rows = samples // dealt_ref.shape[0]
+    weights = columns_of(counts_ref[...])
+    roots = jnp.sqrt(weights)
+
+    def tile(place):
+        return scale_tile(weights, roots, dealt_ref[:, place * rows:(place + 1) * rows, :].reshape(samples, width))
+
+    for position in range(tiles_ref.shape[0]):
+        tiles_ref[position] = tile(position + 1)
+
+    @pl.when(lax.axis_index("col") == 0)
+    def _():
+        right_ref[...] = jnp.concatenate(split(below_ref[...]), axis=0)
+
+    @pl.when(lax.axis_index("col") > 0)
+    def _():
+        keep, level = coefficients(number_ref, over_ref, trace_ref, taps)
+        first_tile = tile(0)
         panel_ref[:, 0:samples] = (keep / level) * dot(first_tile, first_tile, ((1,), (1,))) + identity(samples)
         panel_ref[:, samples:] = identity(samples)
         factor_panel(panel_ref, work_ref, samples)
         inverse_factor = panel_ref[:, samples:]
         parts = jnp.concatenate(split(keep * gram(inverse_factor, 0, samples)), axis=1)
         own = scaled_ref[...]
-        finish(dot(parts, jnp.concatenate([own, own], axis=0), ((1,), (0,))))
-        for position in range(positions):
-            @pl.when(position * sources + row_index == col_index)
-            def _():
-                out_ref[position] = out_ref[position] + level * identity(width)
+        right_ref[...] = jnp.concatenate(split(dot(parts, jnp.concatenate([own, own], axis=0), ((1,), (0,)))), axis=0)
+
+
+def finish_kernel(
+    taps, number_ref, over_ref, trace_ref, counts_ref, right_ref, tiles_ref, diagonal_ref, eight_ref, even_ref, odd_ref, out_ref,
+    held_ref, arrived,
+):
+    positions, samples, width = tiles_ref.shape
+    row_index, col_index = lax.axis_index("row"), lax.axis_index("col")
+    rows_count = lax.axis_size("row")
+
+    def fill(position, tile):
+        out_ref[position] = dot(jnp.concatenate([tile, tile], axis=0), right_ref[...], ((0,), (0,)))
+
+    for position in range(1, positions):
+        fill(position, tiles_ref[position])
+
+    @pl.when((2 * row_index == rows_count))
+    def _():
+        copies_in = [
+            pltpu.make_async_copy(source, held_ref.at[place], arrived.at[place])
+            for place, source in enumerate((eight_ref, even_ref, odd_ref))
+        ]
+        for copy in copies_in:
+            copy.start()
+        for copy in copies_in:
+            copy.wait()
+        weights = columns_of(counts_ref[...])
+        eight = held_ref[0].astype(F32) + held_ref[1].astype(F32) + held_ref[2].astype(F32)
+        fill(0, scale_tile(weights, jnp.sqrt(weights), eight))
+
+    @pl.when((2 * row_index != rows_count) & (row_index > 0))
+    def _():
+        fill(0, tiles_ref[0])
 
     @pl.when((row_index == 0) & (col_index > 0))
     def _():
@@ -227,6 +272,12 @@
     @pl.when((row_index == 0) & (col_index == 0))
     def _():
         out_ref[0] = diagonal_ref[...]
+
+    for position in range(positions):
+        @pl.when((position * rows_count + row_index == col_index) & (col_index > 0))
+        def _():
+            _, level = coefficients(number_ref, over_ref, trace_ref, taps)
+            out_ref[position] = out_ref[position] + level * identity(width)
 
 
 def limit(mebibytes):
@@ -246,7 +297,7 @@
     )(counts[None, :], samples)
 
 
-def scale(counts, gathered, columns):
+def scale(counts, gathered, helped, helped_too, columns):
     count, rows, width = gathered.shape
     return pl.pallas_call(
         scale_kernel,
@@ -254,24 +305,39 @@
             jax.ShapeDtypeStruct((count * rows, width), BF16),
             jax.ShapeDtypeStruct((columns, rows * width // 128 + TAIL, 128), BF16),
         ),
-        in_specs=[VMEM, VMEM],
+        in_specs=[VMEM] * 4,
         out_specs=(VMEM, VMEM),
         compiler_params=limit(16),
-    )(counts, gathered)
+    )(counts, gathered, helped, helped_too)
 
 
 def deal(pieces, rows, width, targets):
-    columns = pieces.shape[0]
     return pl.pallas_call(
         deal_kernel,
         out_shape=(
-            jax.ShapeDtypeStruct((targets, (1 + columns // targets) * rows, width), BF16),
+            jax.ShapeDtypeStruct((targets, 6 * rows, width), BF16),
             jax.ShapeDtypeStruct((8, 128), F32),
         ),
         in_specs=[VMEM],
         out_specs=(VMEM, VMEM),
         compiler_params=limit(16),
     )(pieces)
+
+
+def hold_kernel(_, value_ref, held_ref):
+    count, rows, _ = value_ref.shape
+    held_ref[...] = value_ref[...].reshape(count * rows, -1)
+
+
+def hold(value, after):
+    count, rows, width = value.shape
+    return pl.pallas_call(
+        hold_kernel,
+        out_shape=jax.ShapeDtypeStruct((count * rows, width), BF16),
+        in_specs=[pl.BlockSpec(memory_space=pl.ANY), VMEM],
+        out_specs=VMEM,
+        compiler_params=limit(8),
+    )(after, value)
 
 
 def panel(number, over, trace, scaled, taps):
@@ -293,31 +359,58 @@
     )(number, over, trace, scaled)
 
 
-def tiles(number, over, trace, scaled, below, diagonal, dealt, taps):
+def right_factor(number, over, trace, counts, scaled, below, dealt, taps):
     samples, width = scaled.shape
-    positions = dealt.shape[1] * dealt.shape[0] // samples - 1
-    return pl.pallas_call(
-        functools.partial(tiles_kernel, taps),
-        out_shape=jax.ShapeDtypeStruct((positions, width, width), F32),
+    return pl.pallas_call(
+        functools.partial(right_kernel, taps),
+        out_shape=(
+            jax.ShapeDtypeStruct((2 * samples, width), BF16),
+            jax.ShapeDtypeStruct((2, samples, width), BF16),
+        ),
         in_specs=[SMEM, SMEM] + [VMEM] * 5,
-        out_specs=VMEM,
+        out_specs=(VMEM, VMEM),
         scratch_shapes=[
             pltpu.VMEM((samples, 2 * samples), F32),
             pltpu.VMEM((BLOCK, 2 * BLOCK), F32),
         ],
         compiler_params=limit(32),
-    )(number, over, trace, scaled, below, diagonal, dealt)
-
-
-def near_groups(rows_count, cols_count):
+        cost_estimate=pl.CostEstimate(flops=10**10, bytes_accessed=2 * 2**20, transcendentals=0),
+    )(number, over, trace, counts, scaled, below, dealt)
+
+
+def finish(number, over, trace, counts, right, tiles, diagonal, eights, taps):
+    positions, samples, width = tiles.shape
+    return pl.pallas_call(
+        functools.partial(finish_kernel, taps),
+        out_shape=jax.ShapeDtypeStruct((positions, width, width), F32),
+        in_specs=[SMEM, SMEM] + [VMEM] * 5 + [pl.BlockSpec(memory_space=pl.ANY)] * 3,
+        out_specs=VMEM,
+        scratch_shapes=[pltpu.VMEM((3, samples, width), BF16), pltpu.SemaphoreType.DMA((3,))],
+        compiler_params=limit(32),
+    )(number, over, trace, counts, right, tiles, diagonal, *eights)
+
+
+def helper_pairs(rows_count, cols_count):
+    fine, half_rows = cols_count // COARSE, rows_count // 2
+    pairs, too = [], []
+    for place in range(half_rows):
+        source = (2 * place + 1) * cols_count
+        for tile in range(cols_count):
+            half = tile // fine % 2
+            helper = tile + fine * (1 - 2 * half)
+            if tile != fine:
+                pairs.append((source + tile, (half * half_rows + place) * cols_count + helper))
+        too.append((source, (half_rows + place) * cols_count + fine))
+    return pairs, too
+
+
+def eight_pairs(rows_count, cols_count):
     fine = cols_count // COARSE
-    groups = []
-    for column in range(cols_count):
-        mirrored = (COARSE - 1 - column // fine) * fine + column % fine
-        groups.append(
-            [row * cols_count + (column if 2 * row < rows_count else mirrored) for row in range(rows_count)]
-        )
-    return groups
+    wanted = rows_count // 2 * cols_count
+    first = [(fine, wanted)]
+    return first, [
+        [(row * cols_count + fine, wanted + 2 * row + turn) for row in range(rows_count) if row + turn > 0] for turn in range(2)
+    ]
 
 
 def per_device(samples, counts, shrink_num, shrink_den):
@@ -325,14 +418,23 @@
     cols_count = lax.axis_size("col")
     rows, width = samples.shape
     taps = width * cols_count
+    both = ("row", "col")
+    helped, helped_too = (lax.ppermute(samples, both, pairs) for pairs in helper_pairs(rows_count, cols_count))
     own, counts = copies(counts, samples, rows_count)
     gathered = lax.all_to_all(own, "row", 0, 0)
-    scaled, pieces = scale(counts, gathered, cols_count)
+    scaled, pieces = scale(counts, gathered, helped, helped_too, cols_count)
+    pairs_first, pairs_late = eight_pairs(rows_count, cols_count)
+    eights = [lax.ppermute(gathered.reshape(rows_count * rows, width), both, pairs_first)]
     exchanged = lax.all_to_all(pieces, "col", 0, 0)
-    dealt, trace = deal(exchanged, rows, width, rows_count)
-    dealt = lax.all_to_all(dealt, ("row", "col"), 0, 0, axis_index_groups=near_groups(rows_count, cols_count))
+    half_rows = rows_count // 2
+    dealt, trace = deal(exchanged, rows, width, half_rows)
+    halves = [list(range(half_rows)), list(range(half_rows, rows_count))]
+    dealt = lax.all_to_all(dealt, "row", 0, 0, axis_index_groups=halves)
     below, diagonal = panel(shrink_num, shrink_den, trace, scaled, taps)
-    return tiles(shrink_num, shrink_den, trace, scaled, below, diagonal, dealt, taps)
+    whole = hold(gathered, below)
+    eights += [lax.ppermute(whole, both, pairs) for pairs in pairs_late]
+    right, tiles = right_factor(shrink_num, shrink_den, trace, counts, scaled, below, dealt, taps)
+    return finish(shrink_num, shrink_den, trace, counts, right, tiles, diagonal, eights, taps)
 
 
 def solution(mesh):

time: 94.2 us -> 87.6 us (0.930)
  the two profiles are of different devices: /device:TPU:64 before, /device:TPU:120 now
where the time goes in v5:
time: 87.6 us; the launch traced here: 87 us
  starting transfers between devices  34 us (39%)
  waiting for transfers between devices  33.9 us (39%)
  Pallas kernels  15.2 us (17%)
  local copies, waits for them, and re-layouts  2.35 us (3%)
  between operations  1.56 us (2%)
    all_to_all x1, starting transfers between devices, per_device(): exchanged = lax.all_to_all(pieces, 'col', 0, 0)  15.6 us
    all_to_all x1, waiting for transfers between devices, per_device(): exchanged = lax.all_to_all(pieces, 'col', 0, 0)  15.3 us
    all_to_all x1, waiting for transfers between devices, per_device(): dealt = lax.all_to_all(dealt, 'row', 0, 0, axis_index_groups=halves)  13.1 us
    all_to_all x1, starting transfers between devices, per_device(): gathered = lax.all_to_all(own, 'row', 0, 0)  9.68 us
    pallas_call x1, Pallas kernels, right_factor(): pl.pallas_call(functools.partial(right_kernel, taps), out_shape=(jax.Shap...  8.55 us
    all_to_all x1, waiting for transfers between devices, per_device(): gathered = lax.all_to_all(own, 'row', 0, 0)  5.45 us
    all_to_all x1, starting transfers between devices, per_device(): dealt = lax.all_to_all(dealt, 'row', 0, 0, axis_index_groups=halves)  3.85 us
    pallas_call x1, Pallas kernels, finish(): pl.pallas_call(functools.partial(finish_kernel, taps), out_shape=jax.Shap...  3.55 us
  transfers between devices with their start and end apart: 8, of which 3 were waited for; matrix products, arithmetic and copies ran while one was open for 0% of the time, Pallas kernels for 11%

profile of v5, /device:TPU:120, one launch (start us, length us, event | category | flops | bytes accessed | tf_op | source)
XLA Modules:
  0.0 87.0 jit_solution(16145406728215661153)
XLA Ops:
  0.0 0.7 copy-done
  0.7 0.7 copy-done.1
  1.4 0.7 shard_map.46
  2.1 9.7 %all-to-all-start = ((bf16[16,16,512]{2,1,0:T(8,128)(2,1)}), bf16[16,16,512]{2,1,0:T(8,128)(2,1)S(1)}, u32[]{:S(2)}, u32[]{:S(2)}) async-start(bf16[16,16,512]{2,1,0:T(8,128)(2,1)} %get-tuple-element.16), calls=%async_computation | async-start | bytes 524288 | tf_op jit(solution)/shard_map/all_to_all | solution.py:424
  11.8 0.7 collective-permute-start.1
  12.5 0.7 collective-permute-start
  13.1 0.0 collective-permute-done.1.helped_too_ref
  13.1 0.0 collective-permute-done.helped_ref
  13.2 5.5 %all-to-all-done.samples_ref.value_ref = bf16[16,16,512]{2,1,0:T(8,128)(2,1)S(1)} async-done(((bf16[16,16,512]{2,1,0:T(8,128)(2,1)}), bf16[16,16,512]{2,1,0:T(8,128)(2,1)S(1)}, u32[]{:S(2)}, u32[]{:S(2)}) %all-to-all-start) | async-done | bytes 262176 | tf_op jit(solution)/shard_map/all_to_all | solution.py:424
  18.6 1.4 %shard_map.47 = (bf16[256,512]{1,0:T(8,128)(2,1)S(1)}, bf16[32,72,128]{2,1,0:T(8,128)(2,1)}) custom-call(s32[1,256]{1,0:T(1,128)S(1)} %get-tuple-element.15.counts_ref, bf16[16,16,512]{2,1,0:T(8,128)(2,1)S(1)} %all-to-all-done.samples_ref.value_ref, bf16[16,512]{1,0:T(8,128)(2,1)S(1)} %collective-permute-done.helped_ref, ...), custom_call_target="tpu_custom_call" | custom-call | tf_op jit(solution)/shard_map/pallas_call | solution.py:302
  20.0 15.6 %all-to-all-start.1 = ((bf16[32,72,128]{2,1,0:T(8,128)(2,1)}), bf16[32,72,128]{2,1,0:T(8,128)(2,1)S(1)}, u32[]{:S(2)}, u32[]{:S(2)}) async-start(bf16[32,72,128]{2,1,0:T(8,128)(2,1)} %get-tuple-element.17), calls=%async_computation.1 | async-start | bytes 1179648 | tf_op jit(solution)/shard_map/all_to_all | solution.py:428
  36.9 0.7 collective-permute-start.2
  37.6 15.3 %all-to-all-done.1.pieces_ref = bf16[32,72,128]{2,1,0:T(8,128)(2,1)S(1)} async-done(((bf16[32,72,128]{2,1,0:T(8,128)(2,1)}), bf16[32,72,128]{2,1,0:T(8,128)(2,1)S(1)}, u32[]{:S(2)}, u32[]{:S(2)}) %all-to-all-start.1) | async-done | bytes 589856 | tf_op jit(solution)/shard_map/all_to_all | solution.py:428
  52.9 1.0 %shard_map.48 = (bf16[8,96,512]{2,1,0:T(8,128)(2,1)}, f32[8,128]{1,0:T(8,128)S(1)}) custom-call(bf16[32,72,128]{2,1,0:T(8,128)(2,1)S(1)} %all-to-all-done.1.pieces_ref), custom_call_target="tpu_custom_call" | custom-call | tf_op jit(solution)/shard_map/pallas_call | solution.py:315
  54.0 3.8 %all-to-all-start.2 = ((bf16[8,96,512]{2,1,0:T(8,128)(2,1)}), bf16[8,96,512]{2,1,0:T(8,128)(2,1)S(1)}, u32[]{:S(2)}, u32[]{:S(2)}) async-start(bf16[8,96,512]{2,1,0:T(8,128)(2,1)} %get-tuple-element.21), calls=%async_computation.2 | async-start | bytes 1572864 | tf_op jit(solution)/shard_map/all_to_all | solution.py:432
  57.8 1.5 %collective-permute-start.4 = (bf16[256,512]{1,0:T(8,128)(2,1)S(1)}, bf16[256,512]{1,0:T(8,128)(2,1)S(1)}, u32[]{:S(2)}, u32[]{:S(2)}) collective-permute-start(bf16[256,512]{1,0:T(8,128)(2,1)S(1)} %shard_map.51), channel_id=1, source_target_pairs={{8,257},{40,259},{72,261},{104,263},{136,265},{168,267},{200,269},... | collective-permute-start | bytes 786440 | tf_op jit(solution)/shard_map/ppermute | solution.py:435
  59.3 1.4 %collective-permute-start.3 = (bf16[256,512]{1,0:T(8,128)(2,1)S(1)}, bf16[256,512]{1,0:T(8,128)(2,1)}, u32[]{:S(2)}, u32[]{:S(2)}) collective-permute-start(bf16[256,512]{1,0:T(8,128)(2,1)S(1)} %shard_map.51), channel_id=1, source_target_pairs={{40,258},{72,260},{104,262},{136,264},{168,266},{200,268},{232,270... | collective-permute-start | bytes 786440 | tf_op jit(solution)/shard_map/ppermute | solution.py:435
  60.7 13.1 %all-to-all-done.2.dealt_ref = bf16[8,96,512]{2,1,0:T(8,128)(2,1)S(1)} async-done(((bf16[8,96,512]{2,1,0:T(8,128)(2,1)}), bf16[8,96,512]{2,1,0:T(8,128)(2,1)S(1)}, u32[]{:S(2)}, u32[]{:S(2)}) %all-to-all-start.2) | async-done | bytes 786464 | tf_op jit(solution)/shard_map/all_to_all | solution.py:432
  73.8 0.9 %copy-done.3 = bf16[256,512]{1,0:T(8,128)(2,1)S(1)} copy-done((bf16[256,512]{1,0:T(8,128)(2,1)S(1)}, bf16[256,512]{1,0:T(8,128)(2,1)}, u32[]{:S(2)}) %copy-start.3) | copy-done | bytes 262168
  74.7 8.6 %shard_map.50 = (bf16[512,512]{1,0:T(8,128)(2,1)S(1)}, bf16[2,256,512]{2,1,0:T(8,128)(2,1)S(1)}) custom-call(s32[1]{0:T(128)S(6)} %copy.5.number_ref, s32[1]{0:T(128)S(6)} %copy.6.over_ref, f32[8,128]{1,0:T(8,128)S(1)} %get-tuple-element.18.trace_ref, s32[1,256]{1,0:T(1,128)S(1)} %get-tuple-element.15.counts_ref, bf16[256,512]{1,0:T(8,128)(2,1)S(1)} %copy-done.3, ...), custom_call_target="tpu_custom_call" | custom-call | flops 10000000000 | bytes 2097152 | tf_op jit(solution)/shard_map/pallas_call | solution.py:364
  83.3 0.0 collective-permute-done.2.eight_ref
  83.3 0.0 collective-permute-done.4.odd_ref
  83.3 0.0 collective-permute-done.3.even_ref
  83.3 3.6 %shard_map.52 = f32[2,512,512]{2,1,0:T(8,128)} custom-call(s32[1]{0:T(128)S(6)} %copy.5.number_ref, s32[1]{0:T(128)S(6)} %copy.6.over_ref, f32[8,128]{1,0:T(8,128)S(1)} %get-tuple-element.18.trace_ref, s32[1,256]{1,0:T(1,128)S(1)} %get-tuple-element.15.counts_ref, bf16[512,512]{1,0:T(8,128)(2,1)S(1)} %get-tuple-element.22.right_ref, ...), custom_call_target="tpu_custom_call" | custom-call | tf_op jit(solution)/shard_map/pallas_call | solution.py:383
  (7 shorter events, 0.0 us)
Async XLA Ops:
  0.0 0.7 copy-start
  0.7 0.7 copy-start.1
  2.1 16.5 %all-to-all-start = ((bf16[16,16,512]{2,1,0:T(8,128)(2,1)}), bf16[16,16,512]{2,1,0:T(8,128)(2,1)S(1)}, u32[]{:S(2)}, u32[]{:S(2)}) async-start(bf16[16,16,512]{2,1,0:T(8,128)(2,1)} %get-tuple-element.16), calls=%async_computation | async-start | bytes 524288 | tf_op jit(solution)/shard_map/all_to_all | solution.py:424
  11.8 1.3 %collective-permute-start.1 = (bf16[16,512]{1,0:T(8,128)(2,1)}, bf16[16,512]{1,0:T(8,128)(2,1)S(1)}, u32[]{:S(2)}, u32[]{:S(2)}) collective-permute-start(bf16[16,512]{1,0:T(8,128)(2,1)} %samples_ref.1), channel_id=1, source_target_pairs={{32,264},{96,296},{160,328},{224,360},{288,392},{352,424},{416,456... | collective-permute-start | bytes 49160 | tf_op jit(solution)/shard_map/ppermute | solution.py:422
  12.5 0.7 collective-permute-start
  20.0 37.8 %copy-start.2 = (bf16[256,512]{1,0:T(8,128)(2,1)}, bf16[256,512]{1,0:T(8,128)(2,1)S(1)}, u32[]{:S(2)}) copy-start(bf16[256,512]{1,0:T(8,128)(2,1)S(1)} %get-tuple-element.19.scaled_ref) | copy-start | bytes 786436
  20.0 33.0 %all-to-all-start.1 = ((bf16[32,72,128]{2,1,0:T(8,128)(2,1)}), bf16[32,72,128]{2,1,0:T(8,128)(2,1)S(1)}, u32[]{:S(2)}, u32[]{:S(2)}) async-start(bf16[32,72,128]{2,1,0:T(8,128)(2,1)} %get-tuple-element.17), calls=%async_computation.1 | async-start | bytes 1179648 | tf_op jit(solution)/shard_map/all_to_all | solution.py:428
  36.9 46.4 %collective-permute-start.2 = (bf16[256,512]{1,0:T(8,128)(2,1)S(1)}, bf16[256,512]{1,0:T(8,128)(2,1)S(1)}, u32[]{:S(2)}, u32[]{:S(2)}) collective-permute-start(bf16[256,512]{1,0:T(8,128)(2,1)S(1)} %bitcast.2), channel_id=1, source_target_pairs={{8,256}} | collective-permute-start | bytes 786440 | tf_op jit(solution)/shard_map/ppermute | solution.py:427
  54.0 19.8 %all-to-all-start.2 = ((bf16[8,96,512]{2,1,0:T(8,128)(2,1)}), bf16[8,96,512]{2,1,0:T(8,128)(2,1)S(1)}, u32[]{:S(2)}, u32[]{:S(2)}) async-start(bf16[8,96,512]{2,1,0:T(8,128)(2,1)} %get-tuple-element.21), calls=%async_computation.2 | async-start | bytes 1572864 | tf_op jit(solution)/shard_map/all_to_all | solution.py:432
  57.8 25.5 %collective-permute-start.4 = (bf16[256,512]{1,0:T(8,128)(2,1)S(1)}, bf16[256,512]{1,0:T(8,128)(2,1)S(1)}, u32[]{:S(2)}, u32[]{:S(2)}) collective-permute-start(bf16[256,512]{1,0:T(8,128)(2,1)S(1)} %shard_map.51), channel_id=1, source_target_pairs={{8,257},{40,259},{72,261},{104,263},{136,265},{168,267},{200,269},... | collective-permute-start | bytes 786440 | tf_op jit(solution)/shard_map/ppermute | solution.py:435
  59.3 24.0 %collective-permute-start.3 = (bf16[256,512]{1,0:T(8,128)(2,1)S(1)}, bf16[256,512]{1,0:T(8,128)(2,1)}, u32[]{:S(2)}, u32[]{:S(2)}) collective-permute-start(bf16[256,512]{1,0:T(8,128)(2,1)S(1)} %shard_map.51), channel_id=1, source_target_pairs={{40,258},{72,260},{104,262},{136,264},{168,266},{200,268},{232,270... | collective-permute-start | bytes 786440 | tf_op jit(solution)/shard_map/ppermute | solution.py:435
  73.8 1.0 %copy-start.3 = (bf16[256,512]{1,0:T(8,128)(2,1)S(1)}, bf16[256,512]{1,0:T(8,128)(2,1)}, u32[]{:S(2)}) copy-start(bf16[256,512]{1,0:T(8,128)(2,1)} %copy-done.2) | copy-start | bytes 786436

commit v6 on v5

--- a/solution.py
+++ b/solution.py
@@ -54,8 +54,7 @@
     return dot(stack(thirds(left), LEFT, 1), stack(thirds(right), RIGHT, 0), ((1,), (0,)))
 
 
-def copies_kernel(counts_ref, samples_ref, copies_ref, held_ref):
-    held_ref[...] = counts_ref[...]
+def copies_kernel(samples_ref, copies_ref):
     for target in range(copies_ref.shape[0]):
         copies_ref[target] = samples_ref[...]
 
@@ -73,10 +72,15 @@
     return (jnp.concatenate([roots] * repeats, axis=1) * (values - mean)).astype(BF16)
 
 
-def scale_kernel(counts_ref, samples_ref, helped_ref, helped_too_ref, scaled_ref, pieces_ref):
+def weights_kernel(counts_ref, weights_ref):
+    weights = columns_of(counts_ref[...])
+    weights_ref[0] = weights
+    weights_ref[1] = jnp.sqrt(weights)
+
+
+def scale_kernel(weights_ref, samples_ref, helped_ref, scaled_ref, pieces_ref):
     count, rows, width = samples_ref.shape
-    weights = columns_of(counts_ref[...])
-    scaled = scale_tile(weights, jnp.sqrt(weights), samples_ref[...].reshape(count * rows, width))
+    scaled = scale_tile(weights_ref[0], weights_ref[1], samples_ref[...].reshape(count * rows, width))
     scaled_ref[...] = scaled
     share = jnp.sum(jnp.square(scaled.astype(F32)), axis=0, keepdims=True)
     share = jnp.broadcast_to(jnp.sum(share, axis=1, keepdims=True), (TAIL, 128))
@@ -86,13 +90,14 @@
     tail = jnp.where(line == 0, high.astype(F32), 0.0)
     tail = jnp.where(line == 1, middle.astype(F32), tail)
     tail = jnp.where(line == 2, low.astype(F32), tail).astype(BF16)
-    half, place = lax.axis_index("row") // (count // 2), lax.rem(lax.axis_index("row"), count // 2)
+    row = lax.axis_index("row")
+    half = row // (count // 2)
     column = lax.axis_index("col")
     fine = pieces_ref.shape[0] // COARSE
     own = lax.rem(column // fine, 2) == half
     own = (column == 0) | (own & ((half == 0) | (column != fine)))
-    helped = helped_ref[...].astype(F32) + helped_too_ref[...].astype(F32)
-    sent = jnp.where(own, samples_ref[2 * place].astype(F32), helped).astype(BF16)
+    other_block = samples_ref[lax.rem(row + count // 2, count)].astype(F32)
+    sent = jnp.where(own, other_block, helped_ref[...].astype(F32)).astype(BF16)
     body = pieces_ref.shape[1] - TAIL
     for target in range(pieces_ref.shape[0]):
         for part in range(width // 128):
@@ -106,9 +111,8 @@
     fine = columns // COARSE
     rows = dealt_rows // 6
     half = lax.axis_index("row") // targets
-    first, second = half * fine, (1 - half) * fine
     for target in range(targets):
-        sources = (0, fine, first + target, second + target, first + 2 * fine + target, second + 2 * fine + target)
+        sources = ((1 - half) * fine, half * fine, fine + target, target, 3 * fine + target, 2 * fine + target)
         for place, source in enumerate(sources):
             for part in range(width // 128):
                 dealt_ref[target, place * rows:(place + 1) * rows, part * 128:(part + 1) * 128] = pieces_ref[
@@ -188,6 +192,10 @@
 def panel_kernel(taps, number_ref, over_ref, trace_ref, scaled_ref, below_ref, diagonal_ref, panel_ref, work_ref):
     width = scaled_ref.shape[1]
 
+    @pl.when(lax.axis_index("col") > 0)
+    def _():
+        below_ref[...] = scaled_ref[...].astype(F32)
+
     @pl.when(lax.axis_index("col") == 0)
     def _():
         keep, level = coefficients(number_ref, over_ref, trace_ref, taps)
@@ -203,15 +211,19 @@
 
 
 def right_kernel(
-    taps, number_ref, over_ref, trace_ref, counts_ref, scaled_ref, below_ref, dealt_ref, right_ref, tiles_ref, panel_ref, work_ref
+    taps, number_ref, over_ref, trace_ref, counts_ref, below_ref, dealt_ref, right_ref, tiles_ref, panel_ref, work_ref
 ):
-    samples, width = scaled_ref.shape
+    samples, width = below_ref.shape
     rows = samples // dealt_ref.shape[0]
     weights = columns_of(counts_ref[...])
     roots = jnp.sqrt(weights)
 
     def tile(place):
-        return scale_tile(weights, roots, dealt_ref[:, place * rows:(place + 1) * rows, :].reshape(samples, width))
+        halves = [
+            dealt_ref[:, start:start + rows // 2, :].reshape(samples // 2, width)
+            for start in (place * rows, place * rows + rows // 2)
+        ]
+        return scale_tile(weights, roots, jnp.concatenate(halves, axis=0))
 
     for position in range(tiles_ref.shape[0]):
         tiles_ref[position] = tile(position + 1)
@@ -229,25 +241,44 @@
         factor_panel(panel_ref, work_ref, samples)
         inverse_factor = panel_ref[:, samples:]
         parts = jnp.concatenate(split(keep * gram(inverse_factor, 0, samples)), axis=1)
-        own = scaled_ref[...]
+        own = below_ref[...].astype(BF16)
         right_ref[...] = jnp.concatenate(split(dot(parts, jnp.concatenate([own, own], axis=0), ((1,), (0,)))), axis=0)
 
 
 def finish_kernel(
     taps, number_ref, over_ref, trace_ref, counts_ref, right_ref, tiles_ref, diagonal_ref, eight_ref, even_ref, odd_ref, out_ref,
-    held_ref, arrived,
+    held_ref, made_ref, arrived, sent,
 ):
     positions, samples, width = tiles_ref.shape
     row_index, col_index = lax.axis_index("row"), lax.axis_index("col")
     rows_count = lax.axis_size("row")
-
-    def fill(position, tile):
-        out_ref[position] = dot(jnp.concatenate([tile, tile], axis=0), right_ref[...], ((0,), (0,)))
-
-    for position in range(1, positions):
-        fill(position, tiles_ref[position])
-
-    @pl.when((2 * row_index == rows_count))
+    step = width // 2
+    moves = []
+
+    def fill(position, start, tile):
+        part = tile[:, start:start + step]
+        made_ref[position, start:start + step, :] = dot(jnp.concatenate([part, part], axis=0), right_ref[...], ((0,), (0,)))
+
+    def send(position, start):
+        @pl.when((position * rows_count + row_index == col_index) & (col_index > 0))
+        def _():
+            _, level = coefficients(number_ref, over_ref, trace_ref, taps)
+            made_ref[position, start:start + step, start:start + step] = (
+                made_ref[position, start:start + step, start:start + step] + level * identity(step)
+            )
+        move = pltpu.make_async_copy(
+            made_ref.at[position, pl.ds(start, step)], out_ref.at[position, pl.ds(start, step)], sent.at[position, start // step]
+        )
+        move.start()
+        moves.append(move)
+
+    for start in (0, step):
+        fill(1, start, tiles_ref[1])
+        send(1, start)
+
+    eighth = 2 * row_index == rows_count
+
+    @pl.when(eighth)
     def _():
         copies_in = [
             pltpu.make_async_copy(source, held_ref.at[place], arrived.at[place])
@@ -259,45 +290,57 @@
             copy.wait()
         weights = columns_of(counts_ref[...])
         eight = held_ref[0].astype(F32) + held_ref[1].astype(F32) + held_ref[2].astype(F32)
-        fill(0, scale_tile(weights, jnp.sqrt(weights), eight))
-
-    @pl.when((2 * row_index != rows_count) & (row_index > 0))
-    def _():
-        fill(0, tiles_ref[0])
-
-    @pl.when((row_index == 0) & (col_index > 0))
-    def _():
-        out_ref[0] = jnp.zeros((width, width), F32)
-
-    @pl.when((row_index == 0) & (col_index == 0))
-    def _():
-        out_ref[0] = diagonal_ref[...]
-
-    for position in range(positions):
-        @pl.when((position * rows_count + row_index == col_index) & (col_index > 0))
+        held_ref[0] = scale_tile(weights, jnp.sqrt(weights), eight)
+
+    for start in (0, step):
+        @pl.when(eighth)
         def _():
-            _, level = coefficients(number_ref, over_ref, trace_ref, taps)
-            out_ref[position] = out_ref[position] + level * identity(width)
+            fill(0, start, held_ref[0])
+
+        @pl.when(jnp.logical_not(eighth) & (row_index > 0))
+        def _():
+            fill(0, start, tiles_ref[0])
+
+        @pl.when((row_index == 0) & (col_index > 0))
+        def _():
+            made_ref[0, start:start + step, :] = jnp.zeros((step, width), F32)
+
+        @pl.when((row_index == 0) & (col_index == 0))
+        def _():
+            made_ref[0, start:start + step, :] = diagonal_ref[start:start + step, :]
+
+        send(0, start)
+
+    for move in moves:
+        move.wait()
 
 
 def limit(mebibytes):
     return pltpu.CompilerParams(vmem_limit_bytes=mebibytes * 2**20)
 
 
-def copies(counts, samples, count):
+def copies(samples, count):
     return pl.pallas_call(
         copies_kernel,
-        out_shape=(
-            jax.ShapeDtypeStruct((count, *samples.shape), BF16),
-            jax.ShapeDtypeStruct((1, *counts.shape), counts.dtype),
-        ),
-        in_specs=[VMEM, VMEM],
-        out_specs=(VMEM, VMEM),
+        out_shape=jax.ShapeDtypeStruct((count, *samples.shape), BF16),
+        in_specs=[VMEM],
+        out_specs=VMEM,
         compiler_params=limit(8),
-    )(counts[None, :], samples)
-
-
-def scale(counts, gathered, helped, helped_too, columns):
+    )(samples)
+
+
+def weigh(counts):
+    return pl.pallas_call(
+        weights_kernel,
+        out_shape=jax.ShapeDtypeStruct((2, counts.shape[1], 128), F32),
+        in_specs=[VMEM],
+        out_specs=VMEM,
+        compiler_params=limit(8),
+        cost_estimate=pl.CostEstimate(flops=2 * 10**9, bytes_accessed=2 * 2**20, transcendentals=0),
+    )(counts)
+
+
+def scale(weights, gathered, helped, columns):
     count, rows, width = gathered.shape
     return pl.pallas_call(
         scale_kernel,
@@ -305,10 +348,10 @@
             jax.ShapeDtypeStruct((count * rows, width), BF16),
             jax.ShapeDtypeStruct((columns, rows * width // 128 + TAIL, 128), BF16),
         ),
-        in_specs=[VMEM] * 4,
+        in_specs=[VMEM] * 3,
         out_specs=(VMEM, VMEM),
         compiler_params=limit(16),
-    )(counts, gathered, helped, helped_too)
+    )(weights, gathered, helped)
 
 
 def deal(pieces, rows, width, targets):
@@ -359,15 +402,15 @@
     )(number, over, trace, scaled)
 
 
-def right_factor(number, over, trace, counts, scaled, below, dealt, taps):
-    samples, width = scaled.shape
+def right_factor(number, over, trace, counts, below, dealt, taps):
+    samples, width = below.shape
     return pl.pallas_call(
         functools.partial(right_kernel, taps),
         out_shape=(
             jax.ShapeDtypeStruct((2 * samples, width), BF16),
             jax.ShapeDtypeStruct((2, samples, width), BF16),
         ),
-        in_specs=[SMEM, SMEM] + [VMEM] * 5,
+        in_specs=[SMEM, SMEM] + [VMEM] * 4,
         out_specs=(VMEM, VMEM),
         scratch_shapes=[
             pltpu.VMEM((samples, 2 * samples), F32),
@@ -375,7 +418,7 @@
         ],
         compiler_params=limit(32),
         cost_estimate=pl.CostEstimate(flops=10**10, bytes_accessed=2 * 2**20, transcendentals=0),
-    )(number, over, trace, counts, scaled, below, dealt)
+    )(number, over, trace, counts, below, dealt)
 
 
 def finish(number, over, trace, counts, right, tiles, diagonal, eights, taps):
@@ -384,24 +427,28 @@
         functools.partial(finish_kernel, taps),
         out_shape=jax.ShapeDtypeStruct((positions, width, width), F32),
         in_specs=[SMEM, SMEM] + [VMEM] * 5 + [pl.BlockSpec(memory_space=pl.ANY)] * 3,
-        out_specs=VMEM,
-        scratch_shapes=[pltpu.VMEM((3, samples, width), BF16), pltpu.SemaphoreType.DMA((3,))],
+        out_specs=pl.BlockSpec(memory_space=pl.ANY),
+        scratch_shapes=[
+            pltpu.VMEM((3, samples, width), BF16),
+            pltpu.VMEM((positions, width, width), F32),
+            pltpu.SemaphoreType.DMA((3,)),
+            pltpu.SemaphoreType.DMA((positions, 2)),
+        ],
         compiler_params=limit(32),
     )(number, over, trace, counts, right, tiles, diagonal, *eights)
 
 
 def helper_pairs(rows_count, cols_count):
     fine, half_rows = cols_count // COARSE, rows_count // 2
-    pairs, too = [], []
-    for place in range(half_rows):
-        source = (2 * place + 1) * cols_count
+    pairs = []
+    for row in range(rows_count):
+        half = row // half_rows
         for tile in range(cols_count):
-            half = tile // fine % 2
-            helper = tile + fine * (1 - 2 * half)
-            if tile != fine:
-                pairs.append((source + tile, (half * half_rows + place) * cols_count + helper))
-        too.append((source, (half_rows + place) * cols_count + fine))
-    return pairs, too
+            wanted = tile == 0 or (tile // fine % 2 == half and not (half == 1 and tile == fine))
+            if wanted:
+                helper = tile + fine * (1 - 2 * (tile // fine % 2))
+                pairs.append((row * cols_count + tile, row * cols_count + helper))
+    return pairs
 
 
 def eight_pairs(rows_count, cols_count):
@@ -419,10 +466,10 @@
     rows, width = samples.shape
     taps = width * cols_count
     both = ("row", "col")
-    helped, helped_too = (lax.ppermute(samples, both, pairs) for pairs in helper_pairs(rows_count, cols_count))
-    own, counts = copies(counts, samples, rows_count)
-    gathered = lax.all_to_all(own, "row", 0, 0)
-    scaled, pieces = scale(counts, gathered, helped, helped_too, cols_count)
+    helped = lax.ppermute(samples, both, helper_pairs(rows_count, cols_count))
+    counts = counts[None, :]
+    gathered = lax.all_to_all(copies(samples, rows_count), "row", 0, 0)
+    scaled, pieces = scale(weigh(counts), gathered, helped, cols_count)
     pairs_first, pairs_late = eight_pairs(rows_count, cols_count)
     eights = [lax.ppermute(gathered.reshape(rows_count * rows, width), both, pairs_first)]
     exchanged = lax.all_to_all(pieces, "col", 0, 0)
@@ -433,7 +480,7 @@
     below, diagonal = panel(shrink_num, shrink_den, trace, scaled, taps)
     whole = hold(gathered, below)
     eights += [lax.ppermute(whole, both, pairs) for pairs in pairs_late]
-    right, tiles = right_factor(shrink_num, shrink_den, trace, counts, scaled, below, dealt, taps)
+    right, tiles = right_factor(shrink_num, shrink_den, trace, counts, below, dealt, taps)
     return finish(shrink_num, shrink_den, trace, counts, right, tiles, diagonal, eights, taps)
 
 

time: 87.6 us -> 84.9 us (0.969)
  the two profiles are of different devices: /device:TPU:120 before, /device:TPU:65 now
where the time goes in v6:
time: 84.9 us; the launch traced here: 84.4 us
  starting transfers between devices  34.3 us (40%)
  waiting for transfers between devices  33.1 us (39%)
  Pallas kernels  14.8 us (17%)
  between operations  1.56 us (2%)
    all_to_all x1, waiting for transfers between devices, per_device(): exchanged = lax.all_to_all(pieces, 'col', 0, 0)  15.2 us
    all_to_all x1, starting transfers between devices, per_device(): exchanged = lax.all_to_all(pieces, 'col', 0, 0)  12.6 us
    all_to_all x1, starting transfers between devices, per_device(): gathered = lax.all_to_all(copies(samples, rows_count), 'row', 0, 0)  10.2 us
    all_to_all x1, waiting for transfers between devices, per_device(): dealt = lax.all_to_all(dealt, 'row', 0, 0, axis_index_groups=halves)  10 us
    pallas_call x1, Pallas kernels, right_factor(): pl.pallas_call(functools.partial(right_kernel, taps), out_shape=(jax.Shap...  8.56 us
    all_to_all x1, waiting for transfers between devices, per_device(): gathered = lax.all_to_all(copies(samples, rows_count), 'row', 0, 0)  7.41 us
    all_to_all x1, starting transfers between devices, per_device(): dealt = lax.all_to_all(dealt, 'row', 0, 0, axis_index_groups=halves)  6.24 us
    pallas_call x1, Pallas kernels, finish(): pl.pallas_call(functools.partial(finish_kernel, taps), out_shape=jax.Shap...  2.36 us
  transfers between devices with their start and end apart: 7, of which 4 were waited for; matrix products, arithmetic and copies ran while one was open for 0% of the time, Pallas kernels for 12%

profile of v6, /device:TPU:65, one launch (start us, length us, event | category | flops | bytes accessed | tf_op | source)
XLA Modules:
  0.0 84.4 jit_solution(4897786070785532821)
XLA Ops:
  0.0 1.4 %shard_map.47 = bf16[16,16,512]{2,1,0:T(8,128)(2,1)} custom-call(bf16[16,512]{1,0:T(8,128)(2,1)} %samples_ref.1), custom_call_target="tpu_custom_call" | custom-call | tf_op jit(solution)/shard_map/pallas_call | solution.py:323
  1.4 10.2 %all-to-all-start = ((bf16[16,16,512]{2,1,0:T(8,128)(2,1)}), bf16[16,16,512]{2,1,0:T(8,128)(2,1)S(1)}, u32[]{:S(2)}, u32[]{:S(2)}) async-start(bf16[16,16,512]{2,1,0:T(8,128)(2,1)} %shard_map.47), calls=%async_computation | async-start | bytes 524288 | tf_op jit(solution)/shard_map/all_to_all | solution.py:471
  11.7 2.3 %collective-permute-start = (bf16[16,512]{1,0:T(8,128)(2,1)}, bf16[16,512]{1,0:T(8,128)(2,1)S(1)}, u32[]{:S(2)}, u32[]{:S(2)}) collective-permute-start(bf16[16,512]{1,0:T(8,128)(2,1)} %samples_ref.1), channel_id=1, source_target_pairs={{0,8},{1,9},{2,10},{3,11},{4,12},{5,13},{6,14},{7,15},{16,24},{17,... | collective-permute-start | bytes 49160 | tf_op jit(solution)/shard_map/ppermute | solution.py:469
  14.0 0.0 copy-start
  14.0 0.7 copy-done
  14.7 0.2 shard_map.46.weights_ref
  14.9 0.4 collective-permute-done.helped_ref
  15.4 7.4 %all-to-all-done.samples_ref.value_ref = bf16[16,16,512]{2,1,0:T(8,128)(2,1)S(1)} async-done(((bf16[16,16,512]{2,1,0:T(8,128)(2,1)}), bf16[16,16,512]{2,1,0:T(8,128)(2,1)S(1)}, u32[]{:S(2)}, u32[]{:S(2)}) %all-to-all-start) | async-done | bytes 262176 | tf_op jit(solution)/shard_map/all_to_all | solution.py:471
  22.8 1.1 %shard_map.48 = (bf16[256,512]{1,0:T(8,128)(2,1)S(1)}, bf16[32,72,128]{2,1,0:T(8,128)(2,1)}) custom-call(f32[2,256,128]{2,1,0:T(8,128)S(1)} %shard_map.46.weights_ref, bf16[16,16,512]{2,1,0:T(8,128)(2,1)S(1)} %all-to-all-done.samples_ref.value_ref, bf16[16,512]{1,0:T(8,128)(2,1)S(1)} %collective-permute-done.helped_ref), custom_call_target="tpu_custom_call" | custom-call | tf_op jit(solution)/shard_map/pallas_call | solution.py:345
  23.9 12.6 %all-to-all-start.1 = ((bf16[32,72,128]{2,1,0:T(8,128)(2,1)}), bf16[32,72,128]{2,1,0:T(8,128)(2,1)S(1)}, u32[]{:S(2)}, u32[]{:S(2)}) async-start(bf16[32,72,128]{2,1,0:T(8,128)(2,1)} %get-tuple-element.13), calls=%async_computation.1 | async-start | bytes 1179648 | tf_op jit(solution)/shard_map/all_to_all | solution.py:475
  37.8 0.7 collective-permute-start.1
  38.5 15.2 %all-to-all-done.1.pieces_ref = bf16[32,72,128]{2,1,0:T(8,128)(2,1)S(1)} async-done(((bf16[32,72,128]{2,1,0:T(8,128)(2,1)}), bf16[32,72,128]{2,1,0:T(8,128)(2,1)S(1)}, u32[]{:S(2)}, u32[]{:S(2)}) %all-to-all-start.1) | async-done | bytes 589856 | tf_op jit(solution)/shard_map/all_to_all | solution.py:475
  53.7 1.0 %shard_map.49 = (bf16[8,96,512]{2,1,0:T(8,128)(2,1)}, f32[8,128]{1,0:T(8,128)S(1)}) custom-call(bf16[32,72,128]{2,1,0:T(8,128)(2,1)S(1)} %all-to-all-done.1.pieces_ref), custom_call_target="tpu_custom_call" | custom-call | tf_op jit(solution)/shard_map/pallas_call | solution.py:358
  54.7 6.2 %all-to-all-start.2 = ((bf16[8,96,512]{2,1,0:T(8,128)(2,1)}), bf16[8,96,512]{2,1,0:T(8,128)(2,1)S(1)}, u32[]{:S(2)}, u32[]{:S(2)}) async-start(bf16[8,96,512]{2,1,0:T(8,128)(2,1)} %get-tuple-element.17), calls=%async_computation.2 | async-start | bytes 1572864 | tf_op jit(solution)/shard_map/all_to_all | solution.py:479
  60.9 0.0 copy-start.1
  61.0 0.7 collective-permute-start.3
  61.7 1.5 %collective-permute-start.2 = (bf16[256,512]{1,0:T(8,128)(2,1)S(1)}, bf16[256,512]{1,0:T(8,128)(2,1)}, u32[]{:S(2)}, u32[]{:S(2)}) collective-permute-start(bf16[256,512]{1,0:T(8,128)(2,1)S(1)} %shard_map.52), channel_id=1, source_target_pairs={{40,258},{72,260},{104,262},{136,264},{168,266},{200,268},{232,270... | collective-permute-start | bytes 786440 | tf_op jit(solution)/shard_map/ppermute | solution.py:482
  63.3 10.0 %all-to-all-done.2.dealt_ref = bf16[8,96,512]{2,1,0:T(8,128)(2,1)S(1)} async-done(((bf16[8,96,512]{2,1,0:T(8,128)(2,1)}), bf16[8,96,512]{2,1,0:T(8,128)(2,1)S(1)}, u32[]{:S(2)}, u32[]{:S(2)}) %all-to-all-start.2) | async-done | bytes 786464 | tf_op jit(solution)/shard_map/all_to_all | solution.py:479
  73.3 0.0 copy-done.1
  73.3 8.6 %shard_map.51 = (bf16[512,512]{1,0:T(8,128)(2,1)S(1)}, bf16[2,256,512]{2,1,0:T(8,128)(2,1)S(1)}) custom-call(s32[1]{0:T(128)S(6)} %copy.5.number_ref, s32[1]{0:T(128)S(6)} %copy.6.over_ref, f32[8,128]{1,0:T(8,128)S(1)} %get-tuple-element.14.trace_ref, s32[1,256]{1,0:T(1,128)S(1)} %bitcast.4, f32[256,512]{1,0:T(8,128)S(1)} %get-tuple-element.16.below_ref._, ...), custom_call_target="tpu_custom_call" | custom-call | flops 10000000000 | bytes 2097152 | tf_op jit(solution)/shard_map/pallas_call | solution.py:407
  81.8 0.0 collective-permute-done.1.eight_ref
  81.8 0.0 collective-permute-done.3.odd_ref
  81.9 0.0 collective-permute-done.2.even_ref
  81.9 2.4 %shard_map.53 = f32[2,512,512]{2,1,0:T(8,128)} custom-call(s32[1]{0:T(128)S(6)} %copy.5.number_ref, s32[1]{0:T(128)S(6)} %copy.6.over_ref, f32[8,128]{1,0:T(8,128)S(1)} %get-tuple-element.14.trace_ref, s32[1,256]{1,0:T(1,128)S(1)} %bitcast.5, bf16[512,512]{1,0:T(8,128)(2,1)S(1)} %get-tuple-element.18.right_ref, ...), custom_call_target="tpu_custom_call" | custom-call | tf_op jit(solution)/shard_map/pallas_call | solution.py:426
  (2 shorter events, 0.1 us)
Async XLA Ops:
  1.4 21.3 %all-to-all-start = ((bf16[16,16,512]{2,1,0:T(8,128)(2,1)}), bf16[16,16,512]{2,1,0:T(8,128)(2,1)S(1)}, u32[]{:S(2)}, u32[]{:S(2)}) async-start(bf16[16,16,512]{2,1,0:T(8,128)(2,1)} %shard_map.47), calls=%async_computation | async-start | bytes 524288 | tf_op jit(solution)/shard_map/all_to_all | solution.py:471
  11.7 3.7 %collective-permute-start = (bf16[16,512]{1,0:T(8,128)(2,1)}, bf16[16,512]{1,0:T(8,128)(2,1)S(1)}, u32[]{:S(2)}, u32[]{:S(2)}) collective-permute-start(bf16[16,512]{1,0:T(8,128)(2,1)} %samples_ref.1), channel_id=1, source_target_pairs={{0,8},{1,9},{2,10},{3,11},{4,12},{5,13},{6,14},{7,15},{16,24},{17,... | collective-permute-start | bytes 49160 | tf_op jit(solution)/shard_map/ppermute | solution.py:469
  14.0 0.7 copy-start
  23.9 29.8 %all-to-all-start.1 = ((bf16[32,72,128]{2,1,0:T(8,128)(2,1)}), bf16[32,72,128]{2,1,0:T(8,128)(2,1)S(1)}, u32[]{:S(2)}, u32[]{:S(2)}) async-start(bf16[32,72,128]{2,1,0:T(8,128)(2,1)} %get-tuple-element.13), calls=%async_computation.1 | async-start | bytes 1179648 | tf_op jit(solution)/shard_map/all_to_all | solution.py:475
  37.8 44.0 %collective-permute-start.1 = (bf16[256,512]{1,0:T(8,128)(2,1)S(1)}, bf16[256,512]{1,0:T(8,128)(2,1)S(1)}, u32[]{:S(2)}, u32[]{:S(2)}) collective-permute-start(bf16[256,512]{1,0:T(8,128)(2,1)S(1)} %bitcast.2), channel_id=1, source_target_pairs={{8,256}} | collective-permute-start | bytes 786440 | tf_op jit(solution)/shard_map/ppermute | solution.py:474
  54.7 18.5 %all-to-all-start.2 = ((bf16[8,96,512]{2,1,0:T(8,128)(2,1)}), bf16[8,96,512]{2,1,0:T(8,128)(2,1)S(1)}, u32[]{:S(2)}, u32[]{:S(2)}) async-start(bf16[8,96,512]{2,1,0:T(8,128)(2,1)} %get-tuple-element.17), calls=%async_computation.2 | async-start | bytes 1572864 | tf_op jit(solution)/shard_map/all_to_all | solution.py:479
  60.9 12.3 %copy-start.1 = (s32[256]{0:T(256)S(1)}, s32[256]{0:T(256)}, u32[]{:S(2)}) copy-start(s32[256]{0:T(256)} %param.5) | copy-start | bytes 3076
  61.0 20.8 %collective-permute-start.3 = (bf16[256,512]{1,0:T(8,128)(2,1)S(1)}, bf16[256,512]{1,0:T(8,128)(2,1)S(1)}, u32[]{:S(2)}, u32[]{:S(2)}) collective-permute-start(bf16[256,512]{1,0:T(8,128)(2,1)S(1)} %shard_map.52), channel_id=1, source_target_pairs={{8,257},{40,259},{72,261},{104,263},{136,265},{168,267},{200,269},... | collective-permute-start | bytes 786440 | tf_op jit(solution)/shard_map/ppermute | solution.py:482
  61.7 20.1 %collective-permute-start.2 = (bf16[256,512]{1,0:T(8,128)(2,1)S(1)}, bf16[256,512]{1,0:T(8,128)(2,1)}, u32[]{:S(2)}, u32[]{:S(2)}) collective-permute-start(bf16[256,512]{1,0:T(8,128)(2,1)S(1)} %shard_map.52), channel_id=1, source_target_pairs={{40,258},{72,260},{104,262},{136,264},{168,266},{200,268},{232,270... | collective-permute-start | bytes 786440 | tf_op jit(solution)/shard_map/ppermute | solution.py:482

commit v7 on v6

--- a/solution.py
+++ b/solution.py
@@ -48,6 +48,11 @@
     parts = thirds(value)
     left = stack([part[:, first:last] for part in parts], LEFT, 0)
     return dot(left, stack(parts, RIGHT, 0), ((0,), (0,)))
+
+
+def short_gram(value):
+    parts = split(value)
+    return dot(stack(parts, (0, 0, 1), 0), stack(parts, (0, 1, 0), 0), ((0,), (0,)))
 
 
 def product(left, right):
@@ -225,12 +230,14 @@
         ]
         return scale_tile(weights, roots, jnp.concatenate(halves, axis=0))
 
-    for position in range(tiles_ref.shape[0]):
-        tiles_ref[position] = tile(position + 1)
+    def fill():
+        for position in range(tiles_ref.shape[0]):
+            tiles_ref[position] = tile(position + 1)
 
     @pl.when(lax.axis_index("col") == 0)
     def _():
         right_ref[...] = jnp.concatenate(split(below_ref[...]), axis=0)
+        fill()
 
     @pl.when(lax.axis_index("col") > 0)
     def _():
@@ -239,8 +246,9 @@
         panel_ref[:, 0:samples] = (keep / level) * dot(first_tile, first_tile, ((1,), (1,))) + identity(samples)
         panel_ref[:, samples:] = identity(samples)
         factor_panel(panel_ref, work_ref, samples)
+        fill()
         inverse_factor = panel_ref[:, samples:]
-        parts = jnp.concatenate(split(keep * gram(inverse_factor, 0, samples)), axis=1)
+        parts = jnp.concatenate(split(keep * short_gram(inverse_factor)), axis=1)
         own = below_ref[...].astype(BF16)
         right_ref[...] = jnp.concatenate(split(dot(parts, jnp.concatenate([own, own], axis=0), ((1,), (0,)))), axis=0)
 

time: 84.9 us -> 84.6 us (level)
  the two profiles are of different devices: /device:TPU:65 before, /device:TPU:40 now
where the time goes in v7:
time: 84.6 us; the launch traced here: 84.1 us
  starting transfers between devices  33.1 us (39%)
  waiting for transfers between devices  32.8 us (39%)
  Pallas kernels  15.9 us (19%)
  between operations  1.57 us (2%)
    all_to_all x1, waiting for transfers between devices, per_device(): exchanged = lax.all_to_all(pieces, 'col', 0, 0)  15.2 us
    all_to_all x1, starting transfers between devices, per_device(): exchanged = lax.all_to_all(pieces, 'col', 0, 0)  12.1 us
    all_to_all x1, starting transfers between devices, per_device(): gathered = lax.all_to_all(copies(samples, rows_count), 'row', 0, 0)  9.68 us
    pallas_call x1, Pallas kernels, right_factor(): pl.pallas_call(functools.partial(right_kernel, taps), out_shape=(jax.Shap...  8.19 us
    all_to_all x1, waiting for transfers between devices, per_device(): dealt = lax.all_to_all(dealt, 'row', 0, 0, axis_index_groups=halves)  7.14 us
    ppermute x2, starting transfers between devices, per_device(): eights += [lax.ppermute(whole, both, pairs) for pairs in pairs_late]  5.82 us
    ppermute x1, waiting for transfers between devices, per_device(): helped = lax.ppermute(samples, both, helper_pairs(rows_count, cols_count))  4.63 us
    pallas_call x1, Pallas kernels, finish(): pl.pallas_call(functools.partial(finish_kernel, taps), out_shape=jax.Shap...  3.87 us
  transfers between devices with their start and end apart: 7, of which 5 were waited for; matrix products, arithmetic and copies ran while one was open for 0% of the time, Pallas kernels for 11%

profile of v7, /device:TPU:40, one launch (start us, length us, event | category | flops | bytes accessed | tf_op | source)
XLA Modules:
  0.0 84.1 jit_solution(12260438372077935213)
XLA Ops:
  0.0 1.4 %shard_map.47 = bf16[16,16,512]{2,1,0:T(8,128)(2,1)} custom-call(bf16[16,512]{1,0:T(8,128)(2,1)} %samples_ref.1), custom_call_target="tpu_custom_call" | custom-call | tf_op jit(solution)/shard_map/pallas_call | solution.py:331
  1.4 9.7 %all-to-all-start = ((bf16[16,16,512]{2,1,0:T(8,128)(2,1)}), bf16[16,16,512]{2,1,0:T(8,128)(2,1)S(1)}, u32[]{:S(2)}, u32[]{:S(2)}) async-start(bf16[16,16,512]{2,1,0:T(8,128)(2,1)} %shard_map.47), calls=%async_computation | async-start | bytes 524288 | tf_op jit(solution)/shard_map/all_to_all | solution.py:479
  11.1 1.3 %collective-permute-start = (bf16[16,512]{1,0:T(8,128)(2,1)}, bf16[16,512]{1,0:T(8,128)(2,1)S(1)}, u32[]{:S(2)}, u32[]{:S(2)}) collective-permute-start(bf16[16,512]{1,0:T(8,128)(2,1)} %samples_ref.1), channel_id=1, source_target_pairs={{0,8},{1,9},{2,10},{3,11},{4,12},{5,13},{6,14},{7,15},{16,24},{17,... | collective-permute-start | bytes 49160 | tf_op jit(solution)/shard_map/ppermute | solution.py:477
  12.4 0.0 copy-start
  12.4 0.7 copy-done
  13.1 0.2 shard_map.46.weights_ref
  13.3 4.6 %collective-permute-done.helped_ref = bf16[16,512]{1,0:T(8,128)(2,1)S(1)} collective-permute-done((bf16[16,512]{1,0:T(8,128)(2,1)}, bf16[16,512]{1,0:T(8,128)(2,1)S(1)}, u32[]{:S(2)}, u32[]{:S(2)}) %collective-permute-start) | collective-permute-done | bytes 16416 | tf_op jit(solution)/shard_map/ppermute | solution.py:477
  18.0 2.7 %all-to-all-done.samples_ref.value_ref = bf16[16,16,512]{2,1,0:T(8,128)(2,1)S(1)} async-done(((bf16[16,16,512]{2,1,0:T(8,128)(2,1)}), bf16[16,16,512]{2,1,0:T(8,128)(2,1)S(1)}, u32[]{:S(2)}, u32[]{:S(2)}) %all-to-all-start) | async-done | bytes 262176 | tf_op jit(solution)/shard_map/all_to_all | solution.py:479
  20.7 1.1 %shard_map.48 = (bf16[256,512]{1,0:T(8,128)(2,1)S(1)}, bf16[32,72,128]{2,1,0:T(8,128)(2,1)}) custom-call(f32[2,256,128]{2,1,0:T(8,128)S(1)} %shard_map.46.weights_ref, bf16[16,16,512]{2,1,0:T(8,128)(2,1)S(1)} %all-to-all-done.samples_ref.value_ref, bf16[16,512]{1,0:T(8,128)(2,1)S(1)} %collective-permute-done.helped_ref), custom_call_target="tpu_custom_call" | custom-call | tf_op jit(solution)/shard_map/pallas_call | solution.py:353
  21.9 12.1 %all-to-all-start.1 = ((bf16[32,72,128]{2,1,0:T(8,128)(2,1)}), bf16[32,72,128]{2,1,0:T(8,128)(2,1)S(1)}, u32[]{:S(2)}, u32[]{:S(2)}) async-start(bf16[32,72,128]{2,1,0:T(8,128)(2,1)} %get-tuple-element.13), calls=%async_computation.1 | async-start | bytes 1179648 | tf_op jit(solution)/shard_map/all_to_all | solution.py:483
  35.3 0.7 collective-permute-start.1
  36.0 15.2 %all-to-all-done.1.pieces_ref = bf16[32,72,128]{2,1,0:T(8,128)(2,1)S(1)} async-done(((bf16[32,72,128]{2,1,0:T(8,128)(2,1)}), bf16[32,72,128]{2,1,0:T(8,128)(2,1)S(1)}, u32[]{:S(2)}, u32[]{:S(2)}) %all-to-all-start.1) | async-done | bytes 589856 | tf_op jit(solution)/shard_map/all_to_all | solution.py:483
  51.2 1.0 %shard_map.49 = (bf16[8,96,512]{2,1,0:T(8,128)(2,1)}, f32[8,128]{1,0:T(8,128)S(1)}) custom-call(bf16[32,72,128]{2,1,0:T(8,128)(2,1)S(1)} %all-to-all-done.1.pieces_ref), custom_call_target="tpu_custom_call" | custom-call | tf_op jit(solution)/shard_map/pallas_call | solution.py:366
  52.2 3.5 %all-to-all-start.2 = ((bf16[8,96,512]{2,1,0:T(8,128)(2,1)}), bf16[8,96,512]{2,1,0:T(8,128)(2,1)S(1)}, u32[]{:S(2)}, u32[]{:S(2)}) async-start(bf16[8,96,512]{2,1,0:T(8,128)(2,1)} %get-tuple-element.17), calls=%async_computation.2 | async-start | bytes 1572864 | tf_op jit(solution)/shard_map/all_to_all | solution.py:487
  55.8 0.0 copy-start.1
  55.8 0.1 shard_map.50
  55.9 3.7 %collective-permute-start.3 = (bf16[256,512]{1,0:T(8,128)(2,1)S(1)}, bf16[256,512]{1,0:T(8,128)(2,1)S(1)}, u32[]{:S(2)}, u32[]{:S(2)}) collective-permute-start(bf16[256,512]{1,0:T(8,128)(2,1)S(1)} %shard_map.52), channel_id=1, source_target_pairs={{8,257},{40,259},{72,261},{104,263},{136,265},{168,267},{200,269},... | collective-permute-start | bytes 786440 | tf_op jit(solution)/shard_map/ppermute | solution.py:490
  59.6 2.1 %collective-permute-start.2 = (bf16[256,512]{1,0:T(8,128)(2,1)S(1)}, bf16[256,512]{1,0:T(8,128)(2,1)}, u32[]{:S(2)}, u32[]{:S(2)}) collective-permute-start(bf16[256,512]{1,0:T(8,128)(2,1)S(1)} %shard_map.52), channel_id=1, source_target_pairs={{40,258},{72,260},{104,262},{136,264},{168,266},{200,268},{232,270... | collective-permute-start | bytes 786440 | tf_op jit(solution)/shard_map/ppermute | solution.py:490
  61.7 7.1 %all-to-all-done.2.dealt_ref = bf16[8,96,512]{2,1,0:T(8,128)(2,1)S(1)} async-done(((bf16[8,96,512]{2,1,0:T(8,128)(2,1)}), bf16[8,96,512]{2,1,0:T(8,128)(2,1)S(1)}, u32[]{:S(2)}, u32[]{:S(2)}) %all-to-all-start.2) | async-done | bytes 786464 | tf_op jit(solution)/shard_map/all_to_all | solution.py:487
  68.9 8.2 %shard_map.51 = (bf16[512,512]{1,0:T(8,128)(2,1)S(1)}, bf16[2,256,512]{2,1,0:T(8,128)(2,1)S(1)}) custom-call(s32[1]{0:T(128)S(6)} %copy.5.number_ref, s32[1]{0:T(128)S(6)} %copy.6.over_ref, f32[8,128]{1,0:T(8,128)S(1)} %get-tuple-element.14.trace_ref, s32[1,256]{1,0:T(1,128)S(1)} %bitcast.4, f32[256,512]{1,0:T(8,128)S(1)} %get-tuple-element.16.below_ref._, ...), custom_call_target="tpu_custom_call" | custom-call | flops 10000000000 | bytes 2097152 | tf_op jit(solution)/shard_map/pallas_call | solution.py:415
  77.1 0.0 collective-permute-done.1.eight_ref
  77.1 0.0 collective-permute-done.3.odd_ref
  77.1 3.0 %collective-permute-done.2.even_ref = bf16[256,512]{1,0:T(8,128)(2,1)} collective-permute-done((bf16[256,512]{1,0:T(8,128)(2,1)S(1)}, bf16[256,512]{1,0:T(8,128)(2,1)}, u32[]{:S(2)}, u32[]{:S(2)}) %collective-permute-start.2) | collective-permute-done | bytes 262176 | tf_op jit(solution)/shard_map/ppermute | solution.py:490
  80.0 3.9 %shard_map.53 = f32[2,512,512]{2,1,0:T(8,128)} custom-call(s32[1]{0:T(128)S(6)} %copy.5.number_ref, s32[1]{0:T(128)S(6)} %copy.6.over_ref, f32[8,128]{1,0:T(8,128)S(1)} %get-tuple-element.14.trace_ref, s32[1,256]{1,0:T(1,128)S(1)} %bitcast.5, bf16[512,512]{1,0:T(8,128)(2,1)S(1)} %get-tuple-element.18.right_ref, ...), custom_call_target="tpu_custom_call" | custom-call | tf_op jit(solution)/shard_map/pallas_call | solution.py:434
  (2 shorter events, 0.0 us)
Async XLA Ops:
  1.4 19.3 %all-to-all-start = ((bf16[16,16,512]{2,1,0:T(8,128)(2,1)}), bf16[16,16,512]{2,1,0:T(8,128)(2,1)S(1)}, u32[]{:S(2)}, u32[]{:S(2)}) async-start(bf16[16,16,512]{2,1,0:T(8,128)(2,1)} %shard_map.47), calls=%async_computation | async-start | bytes 524288 | tf_op jit(solution)/shard_map/all_to_all | solution.py:479
  11.1 6.8 %collective-permute-start = (bf16[16,512]{1,0:T(8,128)(2,1)}, bf16[16,512]{1,0:T(8,128)(2,1)S(1)}, u32[]{:S(2)}, u32[]{:S(2)}) collective-permute-start(bf16[16,512]{1,0:T(8,128)(2,1)} %samples_ref.1), channel_id=1, source_target_pairs={{0,8},{1,9},{2,10},{3,11},{4,12},{5,13},{6,14},{7,15},{16,24},{17,... | collective-permute-start | bytes 49160 | tf_op jit(solution)/shard_map/ppermute | solution.py:477
  12.4 0.7 copy-start
  21.9 29.4 %all-to-all-start.1 = ((bf16[32,72,128]{2,1,0:T(8,128)(2,1)}), bf16[32,72,128]{2,1,0:T(8,128)(2,1)S(1)}, u32[]{:S(2)}, u32[]{:S(2)}) async-start(bf16[32,72,128]{2,1,0:T(8,128)(2,1)} %get-tuple-element.13), calls=%async_computation.1 | async-start | bytes 1179648 | tf_op jit(solution)/shard_map/all_to_all | solution.py:483
  35.3 41.8 %collective-permute-start.1 = (bf16[256,512]{1,0:T(8,128)(2,1)S(1)}, bf16[256,512]{1,0:T(8,128)(2,1)S(1)}, u32[]{:S(2)}, u32[]{:S(2)}) collective-permute-start(bf16[256,512]{1,0:T(8,128)(2,1)S(1)} %bitcast.2), channel_id=1, source_target_pairs={{8,256}} | collective-permute-start | bytes 786440 | tf_op jit(solution)/shard_map/ppermute | solution.py:482
  52.2 16.6 %all-to-all-start.2 = ((bf16[8,96,512]{2,1,0:T(8,128)(2,1)}), bf16[8,96,512]{2,1,0:T(8,128)(2,1)S(1)}, u32[]{:S(2)}, u32[]{:S(2)}) async-start(bf16[8,96,512]{2,1,0:T(8,128)(2,1)} %get-tuple-element.17), calls=%async_computation.2 | async-start | bytes 1572864 | tf_op jit(solution)/shard_map/all_to_all | solution.py:487
  55.8 13.1 %copy-start.1 = (s32[256]{0:T(256)S(1)}, s32[256]{0:T(256)}, u32[]{:S(2)}) copy-start(s32[256]{0:T(256)} %param.5) | copy-start | bytes 3076
  55.9 21.2 %collective-permute-start.3 = (bf16[256,512]{1,0:T(8,128)(2,1)S(1)}, bf16[256,512]{1,0:T(8,128)(2,1)S(1)}, u32[]{:S(2)}, u32[]{:S(2)}) collective-permute-start(bf16[256,512]{1,0:T(8,128)(2,1)S(1)} %shard_map.52), channel_id=1, source_target_pairs={{8,257},{40,259},{72,261},{104,263},{136,265},{168,267},{200,269},... | collective-permute-start | bytes 786440 | tf_op jit(solution)/shard_map/ppermute | solution.py:490
  59.6 20.4 %collective-permute-start.2 = (bf16[256,512]{1,0:T(8,128)(2,1)S(1)}, bf16[256,512]{1,0:T(8,128)(2,1)}, u32[]{:S(2)}, u32[]{:S(2)}) collective-permute-start(bf16[256,512]{1,0:T(8,128)(2,1)S(1)} %shard_map.52), channel_id=1, source_target_pairs={{40,258},{72,260},{104,262},{136,264},{168,266},{200,268},{232,270... | collective-permute-start | bytes 786440 | tf_op jit(solution)/shard_map/ppermute | solution.py:490
